TPU v7x, 512 devices: a whole 4x4x16 slice. The times are simulated.
512 devices in a mesh: dp: 32 (over x_hi, z), segment: 16 (over y, x_lo, core).
Axes of the slice: x: 4 (x_hi: 2, x_lo: 2; x = x_hi * 2 + x_lo), y: 4, z: 16, core: 2. Of those that a mesh axis runs over, the one named last changes fastest.
Arguments:
- features: bfloat16 [6144, 640], P('dp'), may hold values from -6 to 6
- timesteps: int32 [96], P('dp'), may hold values from 0 to 999
- text_ids: int32 [96, 64], replicated, may hold values from 0 to 16383
- text_table: bfloat16 [16384, 640], P(('dp', 'segment')), may hold values from -12 to 12
- in_weights: bfloat16 [16, 640, 640], P('segment'), may hold values from -0.25 to 0.25
- out_weights: bfloat16 [16, 640, 640], P('segment'), may hold values from -0.25 to 0.25
- skip_weights: bfloat16 [16, 640, 640], P('segment'), may hold values from -0.25 to 0.25
- cotangent: bfloat16 [6144, 640], P('dp'), may hold values from -0.076171875 to 0.076171875
Outputs:
- in_grads: float32 [16, 640, 640], P('segment', 'dp')
- out_grads: float32 [16, 640, 640], P('segment', 'dp')
- skip_grads: float32 [16, 640, 640], P('segment', 'dp')
All inputs are finite; a program needn't handle non-finite values.
Results may differ from a plain program's by a relative error of at most 0.033.
Values may be sent and summed in bfloat16 or wider, within the bound.
A program may use at most 64 MiB of HBM per device.

v0:
```python
import math

import jax
import jax.numpy as jnp
from jax import lax
from jax.sharding import Mesh
from jax.sharding import PartitionSpec as P

GROUPS = 32
DP_SEGMENT = ("dp_0", "dp_1", "segment")
DP = ("dp_0", "dp_1")


EPSILON = 1e-05


def shifted_2(value, axis, steps):
    count = lax.axis_size(axis)
    initial, last = (max(0, -steps), min(count, count - steps))
    return lax.ppermute(value, axis, [(source, source + steps) for source in range(initial, last)])


def partner(block, axis, bit):
    count = lax.axis_size(axis)
    route = []
    for low in range(count):
        high = low | 1 << bit
        if high != low and high < count:
            route += [(low, high), (high, low)]
    return lax.ppermute(block, axis, route)


def sum_in_order(pieces, axes, order):
    inside = pieces.shape[1:]
    pieces = pieces.reshape(*(lax.axis_size(a) for a in axes), *inside)
    pieces = jnp.moveaxis(pieces, order, range(len(axes))).reshape(-1, *inside)
    for k in order:
        pieces = lax.psum_scatter(pieces, axes[k], scatter_dimension=0, tiled=True)
    return pieces[0]


def in_blocks(array, dim, length):
    dims = array.shape
    pieces = array.reshape(*dims[:dim], length, dims[dim] // length, *dims[dim + 1 :])
    return jnp.moveaxis(pieces, dim, 0)


def scatter_axes(array, axes, order, dim):
    length = lax.axis_size(axes)
    return sum_in_order(in_blocks(array, dim, length), axes, order)


def grouped(vector):
    lead = vector.shape[:-1]
    split = vector.reshape(lead + (GROUPS, vector.shape[-1] // GROUPS))
    total = jnp.sum(split, axis=-1, keepdims=True)
    return jnp.broadcast_to(total, split.shape).reshape(vector.shape)


def normalize(block):
    group_size = block.shape[-2] * (block.shape[-1] // GROUPS)
    center = grouped(jnp.sum(block, axis=-2, keepdims=True)) / group_size
    shifted = block - center
    spread = grouped(jnp.sum(shifted * shifted, axis=-2, keepdims=True)) / group_size
    inv_scale = lax.rsqrt(spread + EPSILON)
    return (shifted * inv_scale, inv_scale)


def normalize_back(d_normed, normed, inv_scale):
    group_size = normed.shape[-2] * (normed.shape[-1] // GROUPS)
    mean_first = grouped(jnp.sum(d_normed, axis=-2, keepdims=True)) / group_size
    mean_second = grouped(jnp.sum(d_normed * normed, axis=-2, keepdims=True)) / group_size
    return inv_scale * (d_normed - mean_first - normed * mean_second)


def matmul(left, weight):
    in_shape = left.shape
    flattened = left.reshape(-1, in_shape[-1])
    product = jnp.dot(flattened, weight, preferred_element_type=jnp.float32)
    return product.reshape(in_shape[:-1] + (weight.shape[1],))


def matmul_transposed(left, weight):
    in_shape = left.shape
    flattened = left.reshape(-1, in_shape[-1])
    product = lax.dot_general(
        flattened, weight, (((1,), (1,)), ((), ())), preferred_element_type=jnp.float32
    )
    return product.reshape(in_shape[:-1] + (weight.shape[0],))


def swish_slope(pre_act):
    sigmoid_val = jax.nn.sigmoid(pre_act)
    return sigmoid_val * (1.0 + pre_act * (1.0 - sigmoid_val))


def encode_core(state_in, weight_in, weight_out, condition):
    current = state_in.astype(jnp.float32)
    normed, inv_scale = normalize(current)
    normed_low = normed.astype(jnp.bfloat16)
    pre_act = matmul(normed_low, weight_in) + condition
    hidden = jax.nn.silu(pre_act).astype(jnp.bfloat16)
    result = (current + matmul(hidden, weight_out)).astype(jnp.bfloat16)
    return (current, normed, inv_scale, normed_low, pre_act, hidden, result)


def encode(state_in, weight_in, weight_out, weight_skip, condition):
    parts = encode_core(state_in, weight_in, weight_out, condition)
    result = parts[6]
    skip_out = matmul(result, weight_skip).astype(jnp.bfloat16)
    return (result, skip_out)


def encode_back(
    state_in, weight_in, weight_out, weight_skip, condition, d_result, d_skip, weight_grad
):
    current, normed, inv_scale, normed_low, pre_act, hidden, result = encode_core(
        state_in, weight_in, weight_out, condition
    )
    d_total = d_result.astype(jnp.float32) + matmul_transposed(d_skip, weight_skip)
    grad_skip = weight_grad(result, d_skip)
    d_total_low = d_total.astype(jnp.bfloat16)
    grad_out = weight_grad(hidden, d_total_low)
    d_act = (matmul_transposed(d_total_low, weight_out) * swish_slope(pre_act)).astype(jnp.bfloat16)
    grad_in = weight_grad(normed_low, d_act)
    d_normed = matmul_transposed(d_act, weight_in)
    d_inputs = (d_total + normalize_back(d_normed, normed, inv_scale)).astype(jnp.bfloat16)
    return (d_inputs, grad_in, grad_out, grad_skip)


def decode_core(state_in, skip_in, weight_in, weight_skip, condition):
    current = state_in.astype(jnp.float32) + matmul(skip_in, weight_skip)
    normed, inv_scale = normalize(current)
    normed_low = normed.astype(jnp.bfloat16)
    pre_act = matmul(normed_low, weight_in) + condition
    hidden = jax.nn.silu(pre_act).astype(jnp.bfloat16)
    return (current, normed, inv_scale, normed_low, pre_act, hidden)


def decode(state_in, skip_in, weight_in, weight_out, weight_skip, condition):
    current, normed, inv_scale, normed_low, pre_act, hidden = decode_core(
        state_in, skip_in, weight_in, weight_skip, condition
    )
    return (current + matmul(hidden, weight_out)).astype(jnp.bfloat16)


def decode_back(
    state_in, skip_in, weight_in, weight_out, weight_skip, condition, d_result, weight_grad
):
    current, normed, inv_scale, normed_low, pre_act, hidden = decode_core(
        state_in, skip_in, weight_in, weight_skip, condition
    )
    grad_out = weight_grad(hidden, d_result)
    d_act = (matmul_transposed(d_result, weight_out) * swish_slope(pre_act)).astype(jnp.bfloat16)
    grad_in = weight_grad(normed_low, d_act)
    d_normed = matmul_transposed(d_act, weight_in)
    d_current = (d_result.astype(jnp.float32) + normalize_back(d_normed, normed, inv_scale)).astype(
        jnp.bfloat16
    )
    grad_skip = weight_grad(skip_in, d_current)
    d_skip = matmul_transposed(d_current, weight_skip).astype(jnp.bfloat16)
    return (d_current, d_skip, grad_in, grad_out, grad_skip)


def time_embedding(steps, channels):
    half_width = channels // 2
    freqs = jnp.exp(-math.log(10000.0) * jnp.arange(half_width, dtype=jnp.float32) / half_width)
    angles = steps.astype(jnp.float32)[:, None] * freqs[None, :]
    return jnp.concatenate([jnp.cos(angles), jnp.sin(angles)], axis=-1)


def local_grad(left, right):
    left_flat = left.reshape(-1, left.shape[-1])
    right_flat = right.reshape(-1, right.shape[-1])
    return lax.dot_general(
        left_flat, right_flat, (((0,), (0,)), ((), ())), preferred_element_type=jnp.float32
    )


def take_slot(buffer, chosen_slot):
    return lax.dynamic_slice_in_dim(buffer, chosen_slot, 1, 0)


def store_slot(buffer, chosen_slot, update, active):
    existing = take_slot(buffer, chosen_slot)
    return lax.dynamic_update_slice_in_dim(
        buffer, jnp.where(active, update, existing), chosen_slot, 0
    )


def pass_up(block):
    return shifted_2(block, "segment", 1)


def pass_down(block):
    return shifted_2(block, "segment", -1)


def mirror(buffer):
    bit_count = lax.axis_size("segment").bit_length() - 1
    bit_order = list(range(bit_count))
    for bit_number in bit_order:
        buffer = partner(buffer, "segment", bit_number)
    return buffer


def on_device(
    features, timesteps, text_ids, text_table, in_weights, out_weights, skip_weights, cotangent
):
    segments = lax.axis_size("segment")
    half_segments = segments // 2
    segment_index = lax.axis_index("segment")
    channels = features.shape[-1]
    micro_count = timesteps.shape[0]
    row_count = features.shape[0] // micro_count
    samples = features.reshape(micro_count, row_count, channels)
    cot_blocks = cotangent.reshape(micro_count, row_count, channels)
    weight_in = in_weights[0]
    weight_out = out_weights[0]
    weight_skip = skip_weights[0]
    vocab_rows = text_table.shape[0]
    first_word = lax.axis_index(DP_SEGMENT) * vocab_rows
    vocab_ids = first_word + lax.iota(jnp.int32, vocab_rows)
    counts = jnp.sum(
        (text_ids[None, :, :] == vocab_ids[:, None, None]).astype(jnp.float32), axis=-1
    )
    partial_sum = (
        lax.dot_general(
            counts.astype(jnp.bfloat16),
            text_table,
            (((0,), (0,)), ((), ())),
            preferred_element_type=jnp.float32,
        )
        / text_ids.shape[1]
    )
    pooled_all = lax.psum(partial_sum, DP_SEGMENT)
    dp_index = lax.axis_index(DP)
    pooled = lax.dynamic_slice_in_dim(pooled_all, dp_index * micro_count, micro_count, 0)
    condition = time_embedding(timesteps, channels) + pooled

    def cond_at(chosen_slot):
        return lax.dynamic_slice_in_dim(condition, chosen_slot, 1, 0)[:, None, :]

    zero_block = jnp.zeros((1, row_count, channels), jnp.bfloat16)
    zero_matrix = jnp.zeros((channels, channels), jnp.float32)
    zero_buffer = jnp.zeros((micro_count, row_count, channels), jnp.bfloat16)

    def slot_of(micro_index):
        return jnp.clip(micro_index, 0, micro_count - 1).astype(jnp.int32)

    def enc_step(moment, loop_state):
        incoming, inputs_buf, skips_buf, bottom_buf = loop_state
        micro_index = moment - segment_index
        active = (segment_index < half_segments) & (micro_index >= 0) & (micro_index < micro_count)
        chosen_slot = slot_of(micro_index)
        entering = jnp.where(segment_index == 0, take_slot(samples, chosen_slot), incoming)
        result, skip_out = lax.cond(
            active,
            lambda: encode(entering, weight_in, weight_out, weight_skip, cond_at(chosen_slot)),
            lambda: (zero_block, zero_block),
        )
        inputs_buf = store_slot(inputs_buf, chosen_slot, entering, active)
        skips_buf = store_slot(skips_buf, chosen_slot, skip_out, active)
        arrived = pass_up(result)
        landed = moment - (half_segments - 1)
        land_ok = (segment_index == half_segments) & (landed >= 0) & (landed < micro_count)
        bottom_buf = store_slot(bottom_buf, slot_of(landed), arrived, land_ok)
        return (arrived, inputs_buf, skips_buf, bottom_buf)

    incoming, inputs_buf, skips_buf, bottom_buf = lax.fori_loop(
        0,
        half_segments + micro_count - 1,
        enc_step,
        (zero_block, zero_buffer, zero_buffer, zero_buffer),
    )
    mirrored = mirror(skips_buf)

    def dec_step(moment, loop_state):
        incoming, inputs_buf = loop_state
        micro_index = moment - (segment_index - half_segments)
        active = (segment_index >= half_segments) & (micro_index >= 0) & (micro_index < micro_count)
        chosen_slot = slot_of(micro_index)
        entering = jnp.where(
            segment_index == half_segments, take_slot(bottom_buf, chosen_slot), incoming
        )
        result = lax.cond(
            active,
            lambda: decode(
                entering,
                take_slot(mirrored, chosen_slot),
                weight_in,
                weight_out,
                weight_skip,
                cond_at(chosen_slot),
            ),
            lambda: zero_block,
        )
        inputs_buf = store_slot(inputs_buf, chosen_slot, entering, active)
        return (pass_up(result), inputs_buf)

    incoming, inputs_buf = lax.fori_loop(
        0, half_segments + micro_count - 2, dec_step, (zero_block, inputs_buf)
    )
    inputs_buf = store_slot(inputs_buf, micro_count - 1, incoming, segment_index == segments - 1)

    def dec_back_step(moment, loop_state):
        incoming, grad_sums, dskip_buf, top_buf = loop_state
        micro_index = moment - (segments - 1 - segment_index)
        active = (segment_index >= half_segments) & (micro_index >= 0) & (micro_index < micro_count)
        chosen_slot = slot_of(micro_index)
        entering = jnp.where(
            segment_index == segments - 1, take_slot(cot_blocks, chosen_slot), incoming
        )

        def dec_run_branch():
            d_current, d_skip, grad_in, grad_out, grad_skip = decode_back(
                take_slot(inputs_buf, chosen_slot),
                take_slot(mirrored, chosen_slot),
                weight_in,
                weight_out,
                weight_skip,
                cond_at(chosen_slot),
                entering,
                local_grad,
            )
            return (d_current, d_skip, (grad_in, grad_out, grad_skip))

        def dec_spare_branch():
            return (zero_block, zero_block, (zero_matrix, zero_matrix, zero_matrix))

        d_current, d_skip, new_grads = lax.cond(active, dec_run_branch, dec_spare_branch)
        grad_sums = tuple((old + new for old, new in zip(grad_sums, new_grads)))
        dskip_buf = store_slot(dskip_buf, chosen_slot, d_skip, active)
        arrived = pass_down(d_current)
        landed = moment - (half_segments - 1)
        land_ok = (segment_index == half_segments - 1) & (landed >= 0) & (landed < micro_count)
        top_buf = store_slot(top_buf, slot_of(landed), arrived, land_ok)
        return (arrived, grad_sums, dskip_buf, top_buf)

    zero_grads = (zero_matrix, zero_matrix, zero_matrix)
    incoming, grad_sums, dskip_buf, top_buf = lax.fori_loop(
        0,
        half_segments + micro_count - 1,
        dec_back_step,
        (zero_block, zero_grads, zero_buffer, zero_buffer),
    )
    skip_grads_in = mirror(dskip_buf)

    def enc_back_compute(moment, incoming, grad_sums):
        micro_index = moment - (half_segments - 1 - segment_index)
        active = (segment_index < half_segments) & (micro_index >= 0) & (micro_index < micro_count)
        chosen_slot = slot_of(micro_index)
        entering = jnp.where(
            segment_index == half_segments - 1, take_slot(top_buf, chosen_slot), incoming
        )

        def enc_run_branch():
            d_inputs, grad_in, grad_out, grad_skip = encode_back(
                take_slot(inputs_buf, chosen_slot),
                weight_in,
                weight_out,
                weight_skip,
                cond_at(chosen_slot),
                entering,
                take_slot(skip_grads_in, chosen_slot),
                local_grad,
            )
            return (d_inputs, (grad_in, grad_out, grad_skip))

        def enc_spare_branch():
            return (zero_block, (zero_matrix, zero_matrix, zero_matrix))

        d_inputs, new_grads = lax.cond(active, enc_run_branch, enc_spare_branch)
        grad_sums = tuple((old + new for old, new in zip(grad_sums, new_grads)))
        return (d_inputs, grad_sums)

    def enc_back_step(moment, loop_state):
        incoming, grad_sums = loop_state
        d_inputs, grad_sums = enc_back_compute(moment, incoming, grad_sums)
        return (pass_down(d_inputs), grad_sums)

    last_moment = half_segments + micro_count - 2
    incoming, grad_sums = lax.fori_loop(0, last_moment, enc_back_step, (zero_block, grad_sums))
    unused_inputs, grad_sums = enc_back_compute(last_moment, incoming, grad_sums)
    grad_in, grad_out, grad_skip = (
        scatter_axes(grad_sums[0].astype(jnp.bfloat16), DP, (1, 0), 0).astype(jnp.float32),
        scatter_axes(grad_sums[1].astype(jnp.bfloat16), DP, (1, 0), 0).astype(jnp.float32),
        scatter_axes(grad_sums[2].astype(jnp.bfloat16), DP, (1, 0), 0).astype(jnp.float32),
    )
    return (grad_in[None], grad_out[None], grad_skip[None])


def solution(mesh):
    split = Mesh(mesh.devices.reshape(2, 16, mesh.shape["segment"]), ("dp_0", "dp_1", "segment"))
    placed = (
        P(DP, None),
        P(DP),
        P(),
        P(DP_SEGMENT, None),
        P("segment", None, None),
        P("segment", None, None),
        P("segment", None, None),
        P(DP, None),
    )
    return jax.shard_map(
        on_device,
        mesh=split,
        in_specs=placed,
        out_specs=(P("segment", DP, None), P("segment", DP, None), P("segment", DP, None)),
        check_vma=False,
    )
```

profile of v0, /device:TPU:6, one launch (start us, length us, event | category | flops | bytes accessed | tf_op | source)
XLA Modules:
  0.0 1408.2 jit_solution(15330290352939357973)
XLA Ops:
  10.1 464.1 %all-reduce.10.cloned.1.call-done = f32[96,640]{1,0:T(8,128)} async-done(((f32[96,640]{1,0:T(8,128)}), f32[96,640]{1,0:T(8,128)}) %all-reduce.10.cloned.1.call-update) | async-done | bytes 245776 | tf_op jit(solution)/shard_map/psum | solution.py:236
  475.9 102.6 %while.85 = (s32[]{:T(128)}, bf16[1,64,640]{2,1,0:T(8,128)(2,1)S(1)}, bf16[3,64,640]{2,1,0:T(8,128)(2,1)}, bf16[3,64,640]{2,1,0:T(8,128)(2,1)S(1)}, bf16[3,64,64...) while((s32[]{:T(128)}, ...), condition=%wide.region_9.10_spmd, body=%wide.region_2.9_spmd.sunk | while | flops 158269488 | bytes 7508455 | solution.py:270
  488.4 7.4 collective-permute-done
  551.4 7.6 collective-permute-start
  562.4 5.8 collective-permute-start
  571.6 5.8 collective-permute-start
  578.5 5.8 collective-permute-start.4
  587.3 8.2 collective-permute-done.5
  595.5 5.2 collective-permute-start.6
  600.7 5.4 collective-permute-done.6
  616.2 70.9 %while.86 = (s32[]{:T(128)}, bf16[1,64,640]{2,1,0:T(8,128)(2,1)S(1)}, bf16[3,64,640]{2,1,0:T(8,128)(2,1)}, s32[]{:T(128)}, pred[]{:T(512)}, /*index=5*/pred[]{:T...) while((s32[]{:T(128)}, ...), condition=%wide.region_17.18_spmd, body=%wide.region_10.17_spmd.sunk | while | flops 158064688 | bytes 3985777 | solution.py:301
  661.9 5.5 collective-permute-start.1
  669.8 8.1 collective-permute-start.1
  680.4 5.8 collective-permute-start.1
  690.7 164.4 %while.88 = (s32[]{:T(128)}, bf16[1,64,640]{2,1,0:T(8,128)(2,1)}, f32[640,640]{1,0:T(8,128)}, f32[640,640]{1,0:T(8,128)S(1)}, f32[640,640]{1,0:T(8,128)}, /*inde...) while((s32[]{:T(128)}, bf16[1,64,640]{2,1,0:T(8,128)(2,1)}, ...), condition=%wide.region_29.30_spmd.clone, body=%wide.region_18.29_spmd.clone.sunk | while | flops 423731232 | bytes 53196112 | solution.py:341
  706.7 5.1 conditional.14
  723.2 5.1 conditional.14
  855.2 5.7 collective-permute-start.8
  864.2 8.2 collective-permute-done.9
  872.4 73.8 %collective-permute-start.10 = (bf16[3,64,640]{2,1,0:T(8,128)(2,1)S(1)}, bf16[3,64,640]{2,1,0:T(8,128)(2,1)S(1)}, u32[]{:S(2)}, u32[]{:S(2)}) collective-permute-start(bf16[3,64,640]{2,1,0:T(8,128)(2,1)S(1)} %collective-permute-done.9), channel_id=1, source_target_pairs={{0,4},{4,0},{1,5},{5,1},{2,6},{6,2},{3,7},{7,3},{8,12},{12,8},{9,1... | collective-permute-start | bytes 737288 | tf_op jit(solution)/shard_map/ppermute | solution.py:30
  946.1 5.7 collective-permute-done.10
  951.8 8.8 collective-permute-start.11
  966.2 209.2 %while.87 = (s32[]{:T(128)}, bf16[1,64,640]{2,1,0:T(8,128)(2,1)}, f32[640,640]{1,0:T(8,128)}, f32[640,640]{1,0:T(8,128)S(1)}, f32[640,640]{1,0:T(8,128)}, /*inde...) while((s32[]{:T(128)}, bf16[1,64,640]{2,1,0:T(8,128)(2,1)}, ...), condition=%wide.region_41.42_spmd, body=%wide.region_30.41_spmd.sunk | while | flops 422993952 | bytes 51476620 | solution.py:383
  1039.4 31.1 %collective-permute-done.2 = bf16[1,64,640]{2,1,0:T(8,128)(2,1)S(1)} collective-permute-done((bf16[1,64,640]{2,1,0:T(8,128)(2,1)}, bf16[1,64,640]{2,1,0:T(8,128)(2,1)S(1)}, u32[]{:S(2)}, u32[]{:S(2)}) %collective-permute-start.2) | collective-permute-done | bytes 81952 | tf_op jit(solution)/shard_map/while/body/eval_jaxpr/ppermute | solution.py:20
  1071.1 16.9 %conditional.13 = (bf16[1,64,640]{2,1,0:T(8,128)(2,1)}, f32[640,640]{1,0:T(8,128)}, f32[640,640]{1,0:T(8,128)}, f32[640,640]{1,0:T(8,128)}) conditional(s32[]{:T(128)} %convert_element_type.400, () %tuple.223, (pred[]{:T(512)}, s32[]{:T(128)}, bf16[3,64,640]{2,1,0:T(8,128)(2,1)}, bf16[1,64,640]{2,1,0:T(8,128)(2,1)}, ...), branch_computations={%region_31.31_spmd, %region_32.40_spmd} | conditional | flops 421765152 | bytes 22968052 | solution.py:373
  1098.1 16.9 %conditional.13 = (bf16[1,64,640]{2,1,0:T(8,128)(2,1)}, f32[640,640]{1,0:T(8,128)}, f32[640,640]{1,0:T(8,128)}, f32[640,640]{1,0:T(8,128)}) conditional(s32[]{:T(128)} %convert_element_type.400, () %tuple.223, (pred[]{:T(512)}, s32[]{:T(128)}, bf16[3,64,640]{2,1,0:T(8,128)(2,1)}, bf16[1,64,640]{2,1,0:T(8,128)(2,1)}, ...), branch_computations={%region_31.31_spmd, %region_32.40_spmd} | conditional | flops 421765152 | bytes 22968052 | solution.py:373
  1125.0 16.9 %conditional.13 = (bf16[1,64,640]{2,1,0:T(8,128)(2,1)}, f32[640,640]{1,0:T(8,128)}, f32[640,640]{1,0:T(8,128)}, f32[640,640]{1,0:T(8,128)}) conditional(s32[]{:T(128)} %convert_element_type.400, () %tuple.223, (pred[]{:T(512)}, s32[]{:T(128)}, bf16[3,64,640]{2,1,0:T(8,128)(2,1)}, bf16[1,64,640]{2,1,0:T(8,128)(2,1)}, ...), branch_computations={%region_31.31_spmd, %region_32.40_spmd} | conditional | flops 421765152 | bytes 22968052 | solution.py:373
  1156.5 10.8 collective-permute-start.2
  1192.6 141.3 %all-reduce.12.cloned.1.call-done = (bf16[32,20,640]{2,0,1:T(8,128)(2,1)}, bf16[32,20,640]{2,0,1:T(8,128)(2,1)}, bf16[32,20,640]{2,0,1:T(8,128)(2,1)}) async-done(((bf16[32,20,640]{2,0,1:T(8,128)(2,1)}, bf16[32,20,640]{2,0,1:T(8,128)(2,1)}, bf16[32,20,640]{2,0,1:T(8,128)(2,1)}), (bf16[32,20,640]{2,0,1:T(8,128)(2,1)}, bf16[32,20,640]{2,0,1:T(8,128)(2,1)}, ...) | async-done | bytes 2457616
  1339.0 13.6 reduce-scatter.13.cloned.1.call-done
  1354.0 22.4 %reduce-scatter.15.cloned.1.call-done = bf16[1,20,640]{2,1,0:T(8,128)(2,1)} async-done(((bf16[2,20,640]{2,1,0:T(8,128)(2,1)}), bf16[1,20,640]{2,1,0:T(8,128)(2,1)}) %reduce-scatter.15.cloned.1.call-update) | async-done | bytes 25616
  1377.8 22.4 %reduce-scatter.17.cloned.1.call-done = bf16[1,20,640]{2,1,0:T(8,128)(2,1)} async-done(((bf16[2,20,640]{2,1,0:T(8,128)(2,1)}), bf16[1,20,640]{2,1,0:T(8,128)(2,1)}) %reduce-scatter.17.cloned.1.call-update) | async-done | bytes 25616
  (660 shorter events, 603.2 us)
Async XLA Ops:
  7.2 467.0 %all-reduce.10.cloned.1.call-start = ((), (), s32[]{:S(2)}) async-start(), calls=%async_computation.3 | async-start | bytes 491520 | tf_op jit(solution)/shard_map/psum | solution.py:236
  9.2 1324.7 %all-reduce.12.cloned.1.call-start = ((), (), s32[]{:S(2)}) async-start(), calls=%async_computation.7 | async-start | bytes 4915200
  486.4 9.4 collective-permute-start
  585.4 10.1 collective-permute-start.5
  595.5 10.6 collective-permute-start.6
  606.1 10.0 collective-permute-start.7
  669.8 9.0 collective-permute-start.1
  695.9 9.3 collective-permute-start.3
  711.9 9.8 collective-permute-start.3
  728.4 9.8 collective-permute-start.3
  744.9 9.8 collective-permute-start.3
  761.4 9.8 collective-permute-start.3
  777.8 9.8 collective-permute-start.3
  794.3 9.8 collective-permute-start.3
  810.8 9.8 collective-permute-start.3
  827.3 9.8 collective-permute-start.3
  843.8 9.8 collective-permute-start.3
  862.2 10.1 collective-permute-start.9
  872.4 79.4 %collective-permute-start.10 = (bf16[3,64,640]{2,1,0:T(8,128)(2,1)S(1)}, bf16[3,64,640]{2,1,0:T(8,128)(2,1)S(1)}, u32[]{:S(2)}, u32[]{:S(2)}) collective-permute-start(bf16[3,64,640]{2,1,0:T(8,128)(2,1)S(1)} %collective-permute-done.9), channel_id=1, source_target_pairs={{0,4},{4,0},{1,5},{5,1},{2,6},{6,2},{3,7},{7,3},{8,12},{12,8},{9,1... | collective-permute-start | bytes 737288 | tf_op jit(solution)/shard_map/ppermute | solution.py:30
  951.8 13.8 collective-permute-start.11
  970.7 8.9 collective-permute-start.2
  985.3 10.2 collective-permute-start.2
  1001.2 8.9 collective-permute-start.2
  1015.8 8.9 collective-permute-start.2
  1030.4 40.0 %collective-permute-start.2 = (bf16[1,64,640]{2,1,0:T(8,128)(2,1)}, bf16[1,64,640]{2,1,0:T(8,128)(2,1)S(1)}, u32[]{:S(2)}, u32[]{:S(2)}) collective-permute-start(bf16[1,64,640]{2,1,0:T(8,128)(2,1)} %get-tuple-element.2126), channel_id=1, source_target_pairs={{1,0},{2,1},{3,2},{4,3},{5,4},{6,5},{7,6},{8,7},{9,8},{10,9},{11,1... | collective-permute-start | bytes 245768 | tf_op jit(solution)/shard_map/while/body/eval_jaxpr/ppermute | solution.py:20
  1088.0 9.5 collective-permute-start.2
  1114.9 9.5 collective-permute-start.2
  1141.9 8.9 collective-permute-start.2
  1156.5 17.8 %collective-permute-start.2 = (bf16[1,64,640]{2,1,0:T(8,128)(2,1)}, bf16[1,64,640]{2,1,0:T(8,128)(2,1)S(1)}, u32[]{:S(2)}, u32[]{:S(2)}) collective-permute-start(bf16[1,64,640]{2,1,0:T(8,128)(2,1)} %get-tuple-element.2126), channel_id=1, source_target_pairs={{1,0},{2,1},{3,2},{4,3},{5,4},{6,5},{7,6},{8,7},{9,8},{10,9},{11,1... | collective-permute-start | bytes 245768 | tf_op jit(solution)/shard_map/while/body/eval_jaxpr/ppermute | solution.py:20
  1190.6 162.0 %reduce-scatter.13.cloned.1.call-start = ((), (), s32[]{:S(2)}) async-start(), calls=%async_computation.4 | async-start | bytes 92160
  1335.6 40.8 %reduce-scatter.15.cloned.1.call-start = ((), (), s32[]{:S(2)}) async-start(), calls=%async_computation.5 | async-start | bytes 92160
  1337.3 62.9 %reduce-scatter.17.cloned.1.call-start = ((), (), s32[]{:S(2)}) async-start(), calls=%async_computation.6 | async-start | bytes 92160
  (96 other events, 336.3 us)
Sparse Core Ops, SparseCore 0:
  13.5 460.6 all-reduce.9
  1190.8 143.1 all-reduce.11
  1336.9 15.6 reduce-scatter.12
  1355.4 20.9 reduce-scatter.14
  1379.2 20.9 reduce-scatter.16
where the time goes:
time: 1420 us; the launch traced here: 1410 us
  waiting for transfers between devices  789 us (56%)
  starting transfers between devices  226 us (16%)
  other arithmetic  209 us (15%)
  local copies, waits for them, and re-layouts  122 us (9%)
  matrix products  46.3 us (3%)
  between operations  14.7 us (1%)
    psum x1, waiting for transfers between devices, on_device(): pooled_all = lax.psum(partial_sum, DP_SEGMENT)  464 us
    unnamed x9, waiting for transfers between devices  200 us
    ppermute x38, starting transfers between devices, shifted_2(): lax.ppermute(value, axis, [(source, source + steps) for source in range(i...  117 us
    ppermute x8, starting transfers between devices, partner(): return lax.ppermute(block, axis, route)  108 us
    ppermute x38, waiting for transfers between devices, shifted_2(): lax.ppermute(value, axis, [(source, source + steps) for source in range(i...  84.9 us
    broadcast_in_dim x51, local copies, waits for them, and re-layouts, on_device(): zero_matrix = jnp.zeros((channels, channels), jnp.float32)  65.6 us
    dynamic_update_slice x60, other arithmetic, store_slot(): lax.dynamic_update_slice_in_dim(buffer, jnp.where(active, update, existin...  64.5 us
    add x27, other arithmetic, enc_back_compute(): grad_sums = tuple((old + new for old, new in zip(grad_sums, new_grads)))  62.6 us
  transfers between devices with their start and end apart: 51, of which 35 were waited for; matrix products, arithmetic and copies ran while one was open for 11% of the time, Pallas kernels for 0%

commit v1 on v0

v1 whole, which is shorter than its diff:
```python
import math

import jax
import jax.numpy as jnp
from jax import lax
from jax.experimental import pallas as pl
from jax.experimental.pallas import tpu as pltpu
from jax.sharding import Mesh
from jax.sharding import PartitionSpec as P

C = 640
ROWS = 64
GROUPS = 32
MB = 3
NZ = 16
BF16 = jnp.bfloat16
F32 = jnp.float32
AXES = ("xh", "z", "y", "xl", "co")
DP = ("xh", "z")
SEG = ("y", "xl", "co")
MESH = pl.DeviceIdType.MESH
EPSILON = 1e-05


def dot(a, b):
    return jnp.dot(a, b, preferred_element_type=F32)


def dot_rhs_t(a, b):
    return lax.dot_general(a, b, (((1,), (1,)), ((), ())), preferred_element_type=F32)


def dot_lhs_t(a, b):
    return lax.dot_general(a, b, (((0,), (0,)), ((), ())), preferred_element_type=F32)


def iota(shape, dim):
    return lax.broadcasted_iota(jnp.int32, shape, dim)


def split(v, terms):
    out = []
    for _ in range(terms):
        part = v.astype(BF16)
        out.append(part)
        v = v - part.astype(F32)
    return out


def group_means(sums, terms, group_matrix):
    parts = [p for s in sums for p in split(s, terms)]
    pad = jnp.zeros((16 - len(parts), C), BF16)
    prod = dot(jnp.concatenate(parts + [pad], axis=0), group_matrix)
    out = []
    for k in range(len(sums)):
        total = prod[k * terms : k * terms + 1]
        for t in range(1, terms):
            total = total + prod[k * terms + t : k * terms + t + 1]
        out.append(total * (1.0 / (ROWS * (C // GROUPS))))
    return out


def normalize(v, group_matrix):
    (mean,) = group_means([jnp.sum(v, axis=0, keepdims=True)], 3, group_matrix)
    shifted = v - mean
    (var,) = group_means([jnp.sum(shifted * shifted, axis=0, keepdims=True)], 2, group_matrix)
    inv = lax.rsqrt(var + EPSILON)
    return shifted * inv, inv


def normalize_back(v, normed, inv, group_matrix):
    m1, m2 = group_means(
        [jnp.sum(v, axis=0, keepdims=True), jnp.sum(v * normed, axis=0, keepdims=True)],
        2,
        group_matrix,
    )
    return inv * (v - m1 - normed * m2)


def landed(ref, sem):
    pltpu.make_async_copy(ref, ref, sem).wait()


def kernel(
    feat,
    te,
    ids,
    table,
    w_in,
    w_out,
    w_skip,
    cot,
    out,
    W,
    cur,
    xbuf,
    dbuf,
    xin,
    din,
    xout,
    skout,
    L,
    R,
    sp,
    inv_std,
    LB,
    RB,
    gmat,
    s1m,
    s2m,
    p0f,
    p0b,
    c1,
    c2s,
    c2,
    c3s,
    c3,
    c4s,
    cnd,
    pm,
    pk,
    m_sp,
    m_rp,
    m_sm,
    m_rm,
    k_sp,
    k_rp,
    k_sm,
    k_rm,
    xe_s,
    xe_r,
    in_sem,
    wl,
    wcs,
    wcr,
    wxs,
    wxr,
    wfs,
    wfr,
    c1s_sem,
    c1r_sem,
    c2s_sem,
    c2r_sem,
    c3s_sem,
    c3r_sem,
    c4s_sem,
    c4r_sem,
    hop_s,
    hop_r,
    sk_s,
    sk_r,
    q_s,
    q_r,
    lp_s,
    lp_r,
    rp_s,
    rp_r,
    m_sps,
    m_rps,
    m_sms,
    m_rms,
    k_sps,
    k_rps,
    k_sms,
    k_rms,
    xe_sem,
):
    xh, z, y = lax.axis_index("xh"), lax.axis_index("z"), lax.axis_index("y")
    xl, co = lax.axis_index("xl"), lax.axis_index("co")
    j = xl * 2 + co
    p = xh * 4 + j
    weights = (w_in, w_out, w_skip)
    sample = jnp.minimum(j, MB - 1)
    worker = j < MB
    zc = 4 * j + y
    collector = z == zc
    yc, jc = z % 4, z // 4

    def remote(src, dst, ssem, rsem, dev):
        return pltpu.make_async_remote_copy(
            src_ref=src,
            dst_ref=dst,
            send_sem=ssem,
            recv_sem=rsem,
            device_id=dev,
            device_id_type=MESH,
        )

    for kind in range(3):
        pltpu.make_async_copy(weights[kind].at[0], W.at[kind, j], wl.at[kind]).start()
    rows = pl.ds(pl.multiple_of(sample * ROWS, ROWS), ROWS)
    pltpu.make_async_copy(feat.at[rows], xbuf, in_sem.at[0]).start()
    pltpu.make_async_copy(cot.at[rows], dbuf, in_sem.at[1]).start()

    barrier = pltpu.get_barrier_semaphore()

    def greet(dev):
        pl.semaphore_signal(barrier, inc=1, device_id=dev, device_id_type=MESH)

    for d in range(1, 8):
        q = (p + d) % 8
        greet((q // 4, z, y, (q // 2) % 2, q % 2))
    for d in range(1, 4):
        greet((xh, z, (y + d) % 4, xl, co))
    greet((xh, (z + 1) % NZ, y, xl, co))
    greet((xh, (z + NZ - 1) % NZ, y, xl, co))

    @pl.when(collector)
    def _():
        def tell(d, carry):
            greet((xh, (z + d) % NZ, y, xl, co))
            return carry

        lax.fori_loop(1, NZ, tell, 0)

    is_jc = j == jc
    is_yc = y == yc
    is_source = jnp.logical_and(is_jc, is_yc)

    @pl.when(jnp.logical_and(worker, jnp.logical_not(is_source)))
    def _():
        greet((xh, z, yc, jc // 2, jc % 2))

    base = ((((xh * NZ + z) * 4 + y) * 4) + j) * table.shape[0]
    tokens = ids[...] - base
    lane = iota((96, 128), 1)

    def count(v, acc):
        hits = jnp.sum(jnp.where(tokens == v, 1.0, 0.0), axis=1, keepdims=True)
        return jnp.where(lane == v, hits, acc)

    counts = lax.fori_loop(0, table.shape[0], count, jnp.zeros((96, 128), F32))
    r128 = iota((128, 96), 0)
    place = jnp.where(r128 % 4 < MB, (r128 // 4) * MB + r128 % 4, -1)
    spread = jnp.where(place == iota((128, 96), 1), 1.0, 0.0).astype(BF16)
    counts = dot(spread, counts.astype(BF16))[:, : table.shape[0]].astype(BF16)
    part = dot(counts, table[...]) * (1.0 / ids.shape[1])
    p0f[...] = part.reshape(8, 16, C)
    p0b[...] = p0f[...].astype(BF16)

    expect = 12 + jnp.where(
        collector, 12 - jnp.where(worker, 1, 0), 1
    )
    pl.semaphore_wait(barrier, expect)

    core_dev = (xh, z, y, xl, 1 - co)
    x_devs = ((xh, z, y, 1 - xl, co), (1 - xh, z, y, 1 - xl, co))
    halves = (pl.ds(0, C // 2), pl.ds(C // 2, C // 2))
    far = 2 * (1 - xl) + co

    def start_weights(kind):
        for h in range(2):
            remote(
                weights[kind].at[0, halves[h]],
                W.at[kind, j, halves[h]],
                wxs.at[kind, h],
                wxr.at[kind, h],
                x_devs[h],
            ).start()
        remote(
            weights[kind].at[0], W.at[kind, j], wcs.at[kind], wcr.at[kind], core_dev
        ).start()

    def relay_weights(kind):
        for h in range(2):
            block = W.at[kind, far, halves[h]]
            landed(block, wxr.at[kind, h])
            remote(block, block, wfs.at[kind, h], wfr.at[kind, h], core_dev).start()

    def wait_weights(kind):
        landed(W.at[kind, 0], wl.at[kind])
        landed(W.at[kind, 0], wcr.at[kind])
        for h in range(2):
            landed(W.at[kind, 0, halves[h]], wfr.at[kind, h])

    for d in range(1, 8):
        q = (p + d) % 8
        remote(
            p0b.at[q],
            c1.at[p],
            c1s_sem.at[d],
            c1r_sem.at[p],
            (q // 4, z, y, (q // 2) % 2, q % 2),
        ).start()
    start_weights(0)
    start_weights(1)

    gmat[...] = jnp.where(
        iota((C, 1), 0) // (C // GROUPS) == iota((1, C), 1) // (C // GROUPS), 1.0, 0.0
    ).astype(BF16)
    col = iota((1, C), 1)
    src1 = (col % 40) // 20 * 320 + (col // 40) * 20 + col % 20
    s1m[...] = jnp.where(iota((C, 1), 0) == src1, 1.0, 0.0).astype(BF16)
    col = iota((1, 768), 1)
    off = col % 48
    src2 = jnp.where(off < 40, off // 20 * 320 + (col // 48) * 20 + off % 20, -1)
    s2m[...] = jnp.where(iota((C, 1), 0) == src2, 1.0, 0.0).astype(BF16)

    acc = p0f[p]
    for d in range(1, 8):
        q = (p + d) % 8
        landed(c1.at[q], c1r_sem.at[q])
        acc = acc + c1[q].astype(F32)
    c2s[...] = acc.astype(BF16)
    for d in range(1, 4):
        remote(
            c2s, c2.at[y], c2s_sem.at[d], c2r_sem.at[y], (xh, z, (y + d) % 4, xl, co)
        ).start()
    for d in range(1, 4):
        q = (y + d) % 4
        landed(c2.at[q], c2r_sem.at[q])
        acc = acc + c2[q].astype(F32)

    @pl.when(jnp.logical_not(collector))
    def _():
        c3s[...] = acc.astype(BF16)
        remote(c3s, c3.at[z], c3s_sem, c3r_sem.at[z], (xh, zc, y, xl, co)).start()

    @pl.when(collector)
    def _():
        def gather(d, total):
            q = (z + d) % NZ
            landed(c3.at[q], c3r_sem.at[q])
            return total + c3[q].astype(F32)

        total = lax.fori_loop(1, NZ, gather, acc)
        row = iota((16, C), 0)
        picked = [
            jnp.sum(jnp.where(row == 4 * y + m, total, 0.0), axis=0, keepdims=True)
            for m in range(MB)
        ]
        c4s[...] = jnp.concatenate(picked + [jnp.zeros((8 - MB, C), F32)], axis=0)

        def give(q, carry):
            qy, qj = q // MB, q % MB

            @pl.when(jnp.logical_not(jnp.logical_and(qy == y, qj == j)))
            def _():
                remote(
                    c4s, cnd, c4s_sem.at[q], c4r_sem, (xh, z, qy, qj // 2, qj % 2)
                ).start()

            return carry

        lax.fori_loop(0, 4 * MB, give, 0)

        @pl.when(worker)
        def _():
            cnd[...] = c4s[...]

    start_weights(2)

    @pl.when(jnp.logical_and(worker, jnp.logical_not(is_source)))
    def _():
        landed(cnd, c4r_sem)

    relay_weights(0)
    relay_weights(1)
    wait_weights(0)
    wait_weights(1)
    landed(xbuf, in_sem.at[0])
    landed(dbuf, in_sem.at[1])

    def condition():
        both = cnd[...] + te[...]
        return jnp.sum(
            jnp.where(iota((8, C), 0) == j, both, 0.0), axis=0, keepdims=True
        )

    def activate(i, v, cond):
        normed, inv = normalize(v, gmat[...])
        low = normed.astype(BF16)
        L[i, 0] = low
        inv_std[i] = jnp.broadcast_to(inv, (8, C))
        act = dot(low, W[0, i]) + cond
        sig = 1.0 / (1.0 + jnp.exp(-act))
        hidden = (act * sig).astype(BF16)
        L[i, 1] = hidden
        sp[i] = sig * (1.0 + act * (1.0 - sig))
        return (v + dot(hidden, W[1, i])).astype(BF16)

    def back(i, d_low, d_full):
        R[i, 1] = d_low
        e = (dot_rhs_t(d_low, W[1, i]) * sp[i]).astype(BF16)
        R[i, 0] = e
        v = dot_rhs_t(e, W[0, i])
        g = normalize_back(v, L[i, 0].astype(F32), inv_std[i, 0:1], gmat[...])
        return (d_full + g).astype(BF16)

    def send_part(buf, i, dst, ssem, rsem):
        @pl.when(i == j)
        def _():
            pltpu.make_async_copy(buf.at[i], dst.at[sample], rsem.at[sample]).start()

        @pl.when(i != j)
        def _():
            remote(
                buf.at[i],
                dst.at[sample],
                ssem.at[i],
                rsem.at[sample],
                (xh, z, y, i // 2, i % 2),
            ).start()

    def done_part(buf, ssem):
        def one(i, carry):
            @pl.when(i != j)
            def _():
                landed(buf.at[i], ssem.at[i])

            return carry

        lax.fori_loop(0, 4, one, 0)

    up = (xh, z, (y + 1) % 4, xl, co)
    down = (xh, z, (y + 3) % 4, xl, co)
    across = (xh, z, 3 - y, xl, co)
    encoder = y < 2

    @pl.when(encoder)
    def _():
        @pl.when(worker)
        def _():
            cond = condition()

            @pl.when(y == 0)
            def _():
                cur[...] = xbuf[...].astype(F32)

            @pl.when(y == 1)
            def _():
                landed(xin, hop_r.at[0])
                cur[...] = xin[...].astype(F32)

            def step(i, carry):
                result = activate(i, cur[...], cond)
                L[i, 2] = result
                cur[...] = result.astype(F32)
                return carry

            lax.fori_loop(0, 4, step, 0)
            remote(L.at[3, 2], xin, hop_s.at[0], hop_r.at[0], up).start()

        relay_weights(2)
        wait_weights(2)

        @pl.when(worker)
        def _():
            def give_skip(n, carry):
                i = 3 - n
                skout[i] = dot(L[i, 2], W[2, i]).astype(BF16)
                remote(
                    skout.at[i], L.at[3 - i, 2], sk_s.at[i], sk_r.at[3 - i], across
                ).start()
                return carry

            lax.fori_loop(0, 4, give_skip, 0)

            def give_left(i, carry):
                send_part(L, i, LB, lp_s, lp_r)
                return carry

            lax.fori_loop(0, 4, give_left, 0)

            landed(din, hop_r.at[1])
            cur[...] = din[...].astype(F32)

            def step_back(n, carry):
                i = 3 - n
                landed(R.at[i, 2], q_r.at[i])
                d_full = cur[...] + dot_rhs_t(R[i, 2], W[2, i])
                d_low = back(i, d_full.astype(BF16), d_full)
                cur[...] = d_low.astype(F32)
                send_part(R, i, RB, rp_s, rp_r)
                return carry

            lax.fori_loop(0, 4, step_back, 0)

            @pl.when(y == 1)
            def _():
                xout[...] = cur[...].astype(BF16)
                remote(xout, din, hop_s.at[1], hop_r.at[1], down).start()

            landed(L.at[3, 2], hop_s.at[0])

            def finish(i, carry):
                landed(skout.at[i], sk_s.at[i])
                return carry

            lax.fori_loop(0, 4, finish, 0)

            @pl.when(y == 1)
            def _():
                landed(xout, hop_s.at[1])

    @pl.when(jnp.logical_not(encoder))
    def _():
        relay_weights(2)
        wait_weights(2)

        @pl.when(worker)
        def _():
            cond = condition()
            landed(xin, hop_r.at[0])
            cur[...] = xin[...].astype(F32)

            def step(i, carry):
                landed(L.at[i, 2], sk_r.at[i])
                v = cur[...] + dot(L[i, 2], W[2, i])
                cur[...] = activate(i, v, cond).astype(F32)
                return carry

            lax.fori_loop(0, 4, step, 0)

            @pl.when(y == 2)
            def _():
                xout[...] = cur[...].astype(BF16)
                remote(xout, xin, hop_s.at[0], hop_r.at[0], up).start()

            def give_left(i, carry):
                send_part(L, i, LB, lp_s, lp_r)
                return carry

            lax.fori_loop(0, 4, give_left, 0)

            @pl.when(y == 3)
            def _():
                cur[...] = dbuf[...].astype(F32)

            @pl.when(y == 2)
            def _():
                landed(din, hop_r.at[1])
                cur[...] = din[...].astype(F32)

            def step_back(n, carry):
                i = 3 - n
                d_full = cur[...]
                g = back(i, d_full.astype(BF16), d_full)
                R[i, 2] = g
                cur[...] = g.astype(F32)
                send_part(R, i, RB, rp_s, rp_r)
                return carry

            lax.fori_loop(0, 4, step_back, 0)
            remote(R.at[0, 2], din, hop_s.at[1], hop_r.at[1], down).start()

            def give_q(i, carry):
                skout[i] = dot_rhs_t(R[i, 2], W[2, i]).astype(BF16)
                remote(
                    skout.at[i], R.at[3 - i, 2], q_s.at[i], q_r.at[3 - i], across
                ).start()
                return carry

            lax.fori_loop(0, 4, give_q, 0)
            landed(R.at[0, 2], hop_s.at[1])

            def finish(i, carry):
                landed(skout.at[i], q_s.at[i])
                return carry

            lax.fori_loop(0, 4, finish, 0)

            @pl.when(y == 2)
            def _():
                landed(xout, hop_s.at[0])

    for m in range(MB):
        landed(LB.at[m], lp_r.at[m])
    for m in range(MB):
        landed(RB.at[m], rp_r.at[m])

    def stacked(ref, kind):
        return jnp.concatenate([ref[m, kind] for m in range(MB)], axis=0)

    left = dot(stacked(LB, 2), s2m[...]).astype(BF16)
    grad = dot_lhs_t(left, stacked(RB, 2))
    for c in range(NZ):
        pk[c] = grad[48 * c : 48 * c + 48]
    for kind in range(2):
        left = dot(stacked(LB, kind), s1m[...]).astype(BF16)
        grad = dot_lhs_t(left, stacked(RB, kind))
        for c in range(NZ):
            pm[c, 40 * kind : 40 * kind + 40] = grad[40 * c : 40 * c + 40]

    after = (xh, (z + 1) % NZ, y, xl, co)
    before = (xh, (z + NZ - 1) % NZ, y, xl, co)
    rings = (
        (pk, k_sp, k_rp, k_sm, k_rm, k_sps, k_rps, k_sms, k_rms),
        (pm, m_sp, m_rp, m_sm, m_rm, m_sps, m_rps, m_sms, m_rms),
    )
    half = NZ // 2

    def plus(ring, t, first):
        own, sbuf, rbuf, _, _, ssem, rsem, _, _ = ring
        total = own[(z + half - t + NZ) % NZ]
        if not first:
            landed(rbuf.at[t - 1], rsem.at[t - 1])
            total = total + rbuf[t - 1].astype(F32)
        sbuf[t] = total.astype(BF16)
        remote(sbuf.at[t], rbuf.at[t], ssem.at[t], rsem.at[t], after).start()

    def minus(ring, t, first):
        own, _, _, sbuf, rbuf, _, _, ssem, rsem = ring
        total = own[(z - half + 1 + t + NZ) % NZ]
        if not first:
            landed(rbuf.at[t - 1], rsem.at[t - 1])
            total = total + rbuf[t - 1].astype(F32)
        sbuf[t] = total.astype(BF16)
        remote(sbuf.at[t], rbuf.at[t], ssem.at[t], rsem.at[t], before).start()

    for ring in rings:
        plus(ring, 0, True)
        minus(ring, 0, True)

    def ring_step(t, carry):
        for ring in rings:
            plus(ring, t, False)
            minus(ring, t, False)
        return carry

    lax.fori_loop(1, half - 1, ring_step, 0)
    for ring in rings:
        plus(ring, half - 1, False)
    totals = []
    for ring in rings:
        own, _, rp, _, rm, _, rps, _, rms = ring
        landed(rp.at[half - 1], rps.at[half - 1])
        landed(rm.at[half - 2], rms.at[half - 2])
        totals.append(own[z] + rp[half - 1].astype(F32) + rm[half - 2].astype(F32))

    total = jnp.concatenate([totals[1], totals[0]], axis=0)
    r = iota((64, 128), 0)
    start = r // 20 * 40 + r % 20

    def choose(side):
        source = jnp.where(r < 60, start + 20 * side, -1)
        return jnp.where(source == iota((64, 128), 1), 1.0, 0.0).astype(BF16)

    xe_s[...] = dot(choose(1 - xh), total.astype(BF16)).astype(BF16)
    exchange = remote(
        xe_s, xe_r, xe_sem.at[0], xe_sem.at[1], (1 - xh, z, y, xl, co)
    )
    exchange.start()
    mine = choose(xh)
    own = sum(dot(mine, piece) for piece in split(total, 2))
    exchange.wait_recv()
    out[...] = own + xe_r[...].astype(F32)

    exchange.wait_send()
    for d in range(1, 8):
        landed(p0b.at[0], c1s_sem.at[d])
    for d in range(1, 4):
        landed(c2s, c2s_sem.at[d])

    @pl.when(jnp.logical_not(collector))
    def _():
        landed(c3s, c3s_sem)

    @pl.when(collector)
    def _():
        def given(q, carry):
            qy, qj = q // MB, q % MB

            @pl.when(jnp.logical_not(jnp.logical_and(qy == y, qj == j)))
            def _():
                landed(c4s, c4s_sem.at[q])

            return carry

        lax.fori_loop(0, 4 * MB, given, 0)

    for kind in range(3):
        landed(W.at[kind, 0], wcs.at[kind])
        for h in range(2):
            landed(W.at[kind, 0, halves[h]], wxs.at[kind, h])
            landed(W.at[kind, 0, halves[h]], wfs.at[kind, h])

    @pl.when(worker)
    def _():
        done_part(L, lp_s)
        done_part(R, rp_s)

    def left_ring(t, carry):
        landed(k_sp.at[t], k_sps.at[t])
        landed(m_sp.at[t], m_sps.at[t])
        return carry

    lax.fori_loop(0, half, left_ring, 0)

    def left_ring_back(t, carry):
        landed(k_sm.at[t], k_sms.at[t])
        landed(m_sm.at[t], m_sms.at[t])
        return carry

    lax.fori_loop(0, half - 1, left_ring_back, 0)


def time_embedding(steps, channels):
    half_width = channels // 2
    freqs = jnp.exp(-math.log(10000.0) * jnp.arange(half_width, dtype=F32) / half_width)
    angles = steps.astype(F32)[:, None] * freqs[None, :]
    return jnp.concatenate([jnp.cos(angles), jnp.sin(angles)], axis=-1)


def on_device(features, timesteps, text_ids, text_table, w_in, w_out, w_skip, cotangent):
    te = jnp.pad(time_embedding(timesteps, C), ((0, 8 - MB), (0, 0)))
    dma = pltpu.SemaphoreType.DMA
    half = NZ // 2

    def bf(*shape):
        return pltpu.VMEM(shape, BF16)

    def f32(*shape):
        return pltpu.VMEM(shape, F32)

    block = (ROWS, C)
    scratch = [
        bf(3, 4, C, C),
        f32(*block),
        bf(*block),
        bf(*block),
        bf(*block),
        bf(*block),
        bf(*block),
        bf(4, *block),
        bf(4, 3, *block),
        bf(4, 3, *block),
        f32(4, *block),
        f32(4, 8, C),
        bf(MB, 3, *block),
        bf(MB, 3, *block),
        bf(C, C),
        bf(C, C),
        bf(C, 768),
        f32(8, 16, C),
        bf(8, 16, C),
        bf(8, 16, C),
        bf(16, C),
        bf(4, 16, C),
        bf(16, C),
        bf(NZ, 16, C),
        f32(8, C),
        f32(8, C),
        f32(NZ, 80, C),
        f32(NZ, 48, C),
        bf(half, 80, C),
        bf(half, 80, C),
        bf(half - 1, 80, C),
        bf(half - 1, 80, C),
        bf(half, 48, C),
        bf(half, 48, C),
        bf(half - 1, 48, C),
        bf(half - 1, 48, C),
        bf(64, C),
        bf(64, C),
        dma((2,)),
        dma((3,)),
        dma((3,)),
        dma((3,)),
        dma((3, 2)),
        dma((3, 2)),
        dma((3, 2)),
        dma((3, 2)),
        dma((8,)),
        dma((8,)),
        dma((4,)),
        dma((4,)),
        dma,
        dma((NZ,)),
        dma((4 * MB,)),
        dma,
        dma((2,)),
        dma((2,)),
        dma((4,)),
        dma((4,)),
        dma((4,)),
        dma((4,)),
        dma((4,)),
        dma((MB,)),
        dma((4,)),
        dma((MB,)),
        dma((half,)),
        dma((half,)),
        dma((half - 1,)),
        dma((half - 1,)),
        dma((half,)),
        dma((half,)),
        dma((half - 1,)),
        dma((half - 1,)),
        dma((2,)),
    ]
    vmem = pl.BlockSpec(memory_space=pltpu.VMEM)
    hbm = pl.BlockSpec(memory_space=pl.ANY)
    grads = pl.pallas_call(
        kernel,
        out_shape=jax.ShapeDtypeStruct((64, C), F32),
        in_specs=[hbm, vmem, vmem, vmem, hbm, hbm, hbm, hbm],
        out_specs=vmem,
        scratch_shapes=scratch,
        compiler_params=pltpu.CompilerParams(
            collective_id=0, has_side_effects=True, vmem_limit_bytes=56 * 2**20
        ),
        name="unet_step",
    )(features, te, text_ids, text_table, w_in, w_out, w_skip, cotangent)
    return tuple(grads[None, 20 * k : 20 * k + 20] for k in range(3))


def solution(mesh):
    split_mesh = Mesh(mesh.devices.reshape(2, NZ, 4, 2, 2), AXES)
    weight = P(SEG, None, None)
    return jax.shard_map(
        on_device,
        mesh=split_mesh,
        in_specs=(
            P(DP, None),
            P(DP),
            P(),
            P(DP + SEG, None),
            weight,
            weight,
            weight,
            P(DP, None),
        ),
        out_specs=(P(SEG, DP, None),) * 3,
        check_vma=False,
    )
```

time: 1420 us -> 160 us (0.11)
  waiting for transfers between devices: 789 us -> 0 us
  starting transfers between devices: 226 us -> 0 us
  other arithmetic: 209 us -> 1.49 us
  Pallas kernels: 0 us -> 153 us
  local copies, waits for them, and re-layouts: 122 us -> 3.66 us
  matrix products: 46.3 us -> 0 us
    psum x1 -> x0, waiting for transfers between devices: 464 us -> none  [on_device(): pooled_all = lax.psum(partial_sum, DP_SEGMENT)]
    ppermute x46 -> x0, starting transfers between devices: 225 us -> none  [the longest x38 117 us: shifted_2(): lax.ppermute(value, axis, [(source, source + steps) for source in range(i...]
    unnamed x9 -> x0, waiting for transfers between devices: 200 us -> none
    pallas_call x0 -> x1, Pallas kernels: none -> 153 us  [on_device(): pl.pallas_call(kernel, out_shape=jax.ShapeDtypeStruct((64, C), F32), in_s...]
    ppermute x46 -> x0, waiting for transfers between devices: 125 us -> none  [the longest x38 84.9 us: shifted_2(): lax.ppermute(value, axis, [(source, source + steps) for source in range(i...]
    add x49 -> x0, other arithmetic: 125 us -> none  [the longest x27 62.6 us: enc_back_compute(): grad_sums = tuple((old + new for old, new in zip(grad_sums, new_grads)))]
    broadcast_in_dim x145 -> x1, local copies, waits for them, and re-layouts: 93.4 us -> 0.92 us  [on_device(): return tuple((grads[None, 20 * k:20 * k + 20] for k in range(3)))]
    dynamic_update_slice x60 -> x0, other arithmetic: 64.5 us -> none  [store_slot(): lax.dynamic_update_slice_in_dim(buffer, jnp.where(active, update, existin...]
  transfers between devices with their start and end apart: 51 -> 0, of which waited for: 35 -> 0; matrix products, arithmetic and copies ran while one was open for 11% -> 0% of each run, Pallas kernels for 0% -> 0%
where the time goes in v1:
time: 160 us; the launch traced here: 159 us
  Pallas kernels  153 us (96%)
  local copies, waits for them, and re-layouts  3.66 us (2%)
    pallas_call x1, Pallas kernels, on_device(): pl.pallas_call(kernel, out_shape=jax.ShapeDtypeStruct((64, C), F32), in_s...  153 us

profile of v1, /device:TPU:6, one launch (start us, length us, event | category | flops | bytes accessed | tf_op | source)
XLA Modules:
  0.0 159.2 jit_solution(14191169774392953010)
XLA Ops:
  0.6 0.0 copy-start
  0.6 0.7 convert_element_type.5
  1.3 0.1 multiply_cosine_fusion
  1.4 0.7 select_maximum_fusion.te
  2.1 0.0 copy-done
  2.1 0.7 copy.11.ids
  2.8 153.4 %unet_step.1 = f32[64,640]{1,0:T(8,128)} custom-call(bf16[192,640]{1,0:T(8,128)(2,1)} %feat.1, f32[8,640]{1,0:T(8,128)} %select_maximum_fusion.te, s32[96,64]{1,0:T(8,128)} %copy.11.ids, bf16[32,640]{1,0:T(8,128)(2,1)} %table.1, bf16[1,640,640]{2,1,0:T(8,128)(2,1)} %w_in.1, bf16[1,640,640]{2,1,0:T(8,128)(2,1)} %w_out.1, bf16[1,640,640]{2,1,0:T(8,128)(2,1)} %w_skip.1, ...), custom_call_target="tpu_custom_call" | custom-call | tf_op jit(solution)/shard_map/unet_step/pallas_call | solution.py:794
  156.3 0.9 slice_bitcast_fusion
  157.2 0.7 copy.14
  157.9 0.7 copy.13
  158.6 0.7 copy.12
  (1 shorter events, 0.0 us)
Async XLA Ops:
  0.6 1.5 copy-start

commit v2 on v1

v2 whole, which is shorter than its diff:
```python
import math

import jax
import jax.numpy as jnp
from jax import lax
from jax.experimental import pallas as pl
from jax.experimental.pallas import tpu as pltpu
from jax.sharding import Mesh
from jax.sharding import PartitionSpec as P

C = 640
ROWS = 64
GROUPS = 32
MB = 3
NZ = 16
BF16 = jnp.bfloat16
F32 = jnp.float32
AXES = ("xh", "z", "y", "xl", "co")
DP = ("xh", "z")
SEG = ("y", "xl", "co")
MESH = pl.DeviceIdType.MESH
EPSILON = 1e-05


def dot(a, b):
    return jnp.dot(a, b, preferred_element_type=F32)


def dot_rhs_t(a, b):
    return lax.dot_general(a, b, (((1,), (1,)), ((), ())), preferred_element_type=F32)


def dot_lhs_t(a, b):
    return lax.dot_general(a, b, (((0,), (0,)), ((), ())), preferred_element_type=F32)


def iota(shape, dim):
    return lax.broadcasted_iota(jnp.int32, shape, dim)


def split(v, terms):
    out = []
    for _ in range(terms):
        part = v.astype(BF16)
        out.append(part)
        v = v - part.astype(F32)
    return out


def group_means(sums, terms, group_matrix):
    parts = [p for s in sums for p in split(s, terms)]
    pad = jnp.zeros((16 - len(parts), C), BF16)
    prod = dot(jnp.concatenate(parts + [pad], axis=0), group_matrix)
    out = []
    for k in range(len(sums)):
        total = prod[k * terms : k * terms + 1]
        for t in range(1, terms):
            total = total + prod[k * terms + t : k * terms + t + 1]
        out.append(total * (1.0 / (ROWS * (C // GROUPS))))
    return out


def normalize(v, group_matrix):
    (mean,) = group_means([jnp.sum(v, axis=0, keepdims=True)], 3, group_matrix)
    shifted = v - mean
    (var,) = group_means([jnp.sum(shifted * shifted, axis=0, keepdims=True)], 2, group_matrix)
    inv = lax.rsqrt(var + EPSILON)
    return shifted * inv, inv


def normalize_back(v, normed, inv, group_matrix):
    m1, m2 = group_means(
        [jnp.sum(v, axis=0, keepdims=True), jnp.sum(v * normed, axis=0, keepdims=True)],
        2,
        group_matrix,
    )
    return inv * (v - m1 - normed * m2)


def landed(ref, sem):
    pltpu.make_async_copy(ref, ref, sem).wait()


def kernel(
    steps,
    feat,
    ids_in,
    table_in,
    w_in,
    w_out,
    w_skip,
    cot,
    out_a,
    out_b,
    ids,
    table,
    W,
    cur,
    xbuf,
    dbuf,
    xin,
    din,
    xout,
    skout,
    pre,
    L,
    R,
    sp,
    inv_std,
    LB,
    RB,
    LP,
    gmat,
    s_low,
    s_high,
    p0f,
    p0b,
    c1,
    c2s,
    c2,
    c3s,
    c3,
    pm,
    sbp,
    rbp,
    sbm,
    rbm,
    lastp,
    lastm,
    cross,
    fin,
    in_sem,
    wl,
    wcs,
    wcr,
    wxs,
    wxr,
    wfs,
    wfr,
    c1s_sem,
    c1r_sem,
    c2s_sem,
    c2r_sem,
    c3s_sem,
    c3r_sem,
    hop_s,
    hop_r,
    sk_s,
    sk_r,
    q_s,
    q_r,
    lp_s,
    lp_r,
    rp_s,
    rp_r,
    sps,
    rps,
    sms,
    rms,
    fin_s,
    fin_r,
):
    xh, z, y = lax.axis_index("xh"), lax.axis_index("z"), lax.axis_index("y")
    xl, co = lax.axis_index("xl"), lax.axis_index("co")
    j = xl * 2 + co
    p = xh * 4 + j
    weights = (w_in, w_out, w_skip)
    sample = jnp.minimum(j, MB - 1)
    worker = j < MB
    def remote(src, dst, ssem, rsem, dev):
        return pltpu.make_async_remote_copy(
            src_ref=src,
            dst_ref=dst,
            send_sem=ssem,
            recv_sem=rsem,
            device_id=dev,
            device_id_type=MESH,
        )

    for kind in range(3):
        pltpu.make_async_copy(weights[kind].at[0], W.at[kind, j], wl.at[kind]).start()
    pltpu.make_async_copy(ids_in, ids, in_sem.at[2]).start()
    pltpu.make_async_copy(table_in, table, in_sem.at[3]).start()
    rows = pl.ds(pl.multiple_of(sample * ROWS, ROWS), ROWS)
    pltpu.make_async_copy(feat.at[rows], xbuf, in_sem.at[0]).start()
    pltpu.make_async_copy(cot.at[rows], dbuf, in_sem.at[1]).start()

    barrier = pltpu.get_barrier_semaphore()

    def greet(dev):
        pl.semaphore_signal(barrier, inc=1, device_id=dev, device_id_type=MESH)

    for d in range(1, 8):
        q = (p + d) % 8
        greet((q // 4, z, y, (q // 2) % 2, q % 2))
    for d in range(1, 4):
        greet((xh, z, (y + d) % 4, xl, co))
    for side in (1, NZ - 1):
        greet((1 - xh, (z + side) % NZ, y, xl, co))

    def greet_z(d, carry):
        greet((xh, (z + d) % NZ, y, xl, co))
        return carry

    lax.fori_loop(1, NZ, greet_z, 0)

    landed(ids, in_sem.at[2])
    landed(table, in_sem.at[3])
    base = ((((xh * NZ + z) * 4 + y) * 4) + j) * table.shape[0]
    tokens = ids[...] - base
    words = table.shape[0]
    row = iota((words, 96), 0)

    def count(n, acc):
        for u in range(8):
            v = n * 8 + u
            hits = jnp.sum(jnp.where(tokens == v, 1.0, 0.0), axis=0, keepdims=True)
            acc = jnp.where(row == v, hits, acc)
        return acc

    counts = lax.fori_loop(0, words // 8, count, jnp.zeros((words, 96), F32))
    r96 = iota((1, 96), 1)
    place = (r96 // 48) * 48 + (r96 % 16) * MB + (r96 % 48) // 16
    order = jnp.where(place == iota((96, 1), 0), 1.0, 0.0).astype(BF16)
    counts = dot(counts.astype(BF16), order).astype(BF16)
    part = dot_lhs_t(counts, table[...]) * (1.0 / ids.shape[0])
    p0f[...] = part.reshape(2 * MB, 16, C)
    p0b[...] = p0f[...].astype(BF16)

    pl.semaphore_wait(barrier, 7 + 3 + 2 + NZ - 1)

    core_dev = (xh, z, y, xl, 1 - co)
    x_devs = ((xh, z, y, 1 - xl, co), (1 - xh, z, y, 1 - xl, co))
    halves = (pl.ds(0, C // 2), pl.ds(C // 2, C // 2))
    far = 2 * (1 - xl) + co

    def start_weights(kind):
        for h in range(2):
            remote(
                weights[kind].at[0, halves[h]],
                W.at[kind, j, halves[h]],
                wxs.at[kind, h],
                wxr.at[kind, h],
                x_devs[h],
            ).start()
        remote(
            weights[kind].at[0], W.at[kind, j], wcs.at[kind], wcr.at[kind], core_dev
        ).start()

    def relay_weights(kind):
        for h in range(2):
            block = W.at[kind, far, halves[h]]
            landed(block, wxr.at[kind, h])
            remote(block, block, wfs.at[kind, h], wfr.at[kind, h], core_dev).start()

    def wait_weights(kind):
        landed(W.at[kind, 0], wl.at[kind])
        landed(W.at[kind, 0], wcr.at[kind])
        for h in range(2):
            landed(W.at[kind, 0, halves[h]], wfr.at[kind, h])

    for b in range(2 * MB):
        bx, bj = b // MB, b % MB

        @pl.when(p != 4 * bx + bj)
        def _():
            remote(
                p0b.at[b],
                c1.at[p],
                c1s_sem.at[b],
                c1r_sem.at[p],
                (bx, z, y, bj // 2, bj % 2),
            ).start()

    start_weights(0)
    start_weights(1)
    gmat[...] = jnp.where(
        iota((C, 1), 0) // (C // GROUPS) == iota((1, C), 1) // (C // GROUPS), 1.0, 0.0
    ).astype(BF16)

    @pl.when(worker)
    def _():
        acc = p0f[xh * MB + sample]
        for d in range(1, 8):
            q = (p + d) % 8
            landed(c1.at[q], c1r_sem.at[q])
            acc = acc + c1[q].astype(F32)
        c2s[...] = acc.astype(BF16)
        for d in range(1, 4):
            remote(
                c2s, c2.at[y], c2s_sem.at[d], c2r_sem.at[y], (xh, z, (y + d) % 4, xl, co)
            ).start()
        for d in range(1, 4):
            q = (y + d) % 4
            landed(c2.at[q], c2r_sem.at[q])
            acc = acc + c2[q].astype(F32)
        for r in range(NZ):
            c3s[r] = acc[r : r + 1]

        def give(d, carry):
            q = (z + d) % NZ
            remote(
                c3s.at[q], c3.at[z], c3s_sem.at[q], c3r_sem.at[z], (xh, q, y, xl, co)
            ).start()
            return carry

        lax.fori_loop(1, NZ, give, 0)

    start_weights(2)
    relay_weights(0)
    relay_weights(1)

    @pl.when(y > 0)
    def _():
        relay_weights(2)

    landed(xbuf, in_sem.at[0])
    landed(dbuf, in_sem.at[1])

    def condition():
        lane = iota((1, C), 1)
        half_width = C // 2
        k = jnp.where(lane < half_width, lane, lane - half_width).astype(F32)
        freqs = jnp.exp(-math.log(10000.0) * k / half_width)
        angles = steps[sample].astype(F32) * freqs
        total = jnp.where(lane < half_width, jnp.cos(angles), jnp.sin(angles)) + c3s[z]

        def add(d, acc):
            q = (z + d) % NZ
            landed(c3.at[q], c3r_sem.at[q])
            return acc + c3[q]

        return lax.fori_loop(1, NZ, add, total)


    def startup_sent():
        for b in range(2 * MB):
            bx, bj = b // MB, b % MB

            @pl.when(p != 4 * bx + bj)
            def _():
                landed(p0b.at[0], c1s_sem.at[b])

        @pl.when(worker)
        def _():
            for d in range(1, 4):
                landed(c2s, c2s_sem.at[d])

            def given(d, carry):
                q = (z + d) % NZ
                landed(c3s.at[q], c3s_sem.at[q])
                return carry

            lax.fori_loop(1, NZ, given, 0)

        for kind in range(3):
            landed(W.at[kind, 0], wcs.at[kind])
            for h in range(2):
                landed(W.at[kind, 0, halves[h]], wxs.at[kind, h])
                landed(W.at[kind, 0, halves[h]], wfs.at[kind, h])

    def chain_sent():
        startup_sent()

        @pl.when(worker)
        def _():
            done_part(L, lp_s)
            done_part(R, rp_s)

            def sent(i, carry):
                @pl.when(encoder)
                def _():
                    landed(skout.at[i], sk_s.at[i])

                @pl.when(jnp.logical_not(encoder))
                def _():
                    landed(skout.at[i], q_s.at[i])

                return carry

            lax.fori_loop(0, 4, sent, 0)

            @pl.when(y < 3)
            def _():
                landed(xout, hop_s.at[0])

            @pl.when(y > 0)
            def _():
                landed(xout, hop_s.at[1])

    def activate(i, v, cond):
        normed, inv = normalize(v, gmat[...])
        low = normed.astype(BF16)
        L[i, 0] = low
        inv_std[i] = jnp.broadcast_to(inv, (8, C))
        act = dot(low, W[0, i]) + cond
        sig = 1.0 / (1.0 + jnp.exp(-act))
        hidden = (act * sig).astype(BF16)
        L[i, 1] = hidden
        sp[i] = sig * (1.0 + act * (1.0 - sig))
        return (v + dot(hidden, W[1, i])).astype(BF16)

    def back(i, d_low, d_full):
        R[i, 1] = d_low
        e = (dot_rhs_t(d_low, W[1, i]) * sp[i]).astype(BF16)
        R[i, 0] = e
        v = dot_rhs_t(e, W[0, i])
        g = normalize_back(v, L[i, 0].astype(F32), inv_std[i, 0:1], gmat[...])
        return (d_full + g).astype(BF16)

    def send_part(buf, i, dst, ssem, rsem):
        @pl.when(i == j)
        def _():
            pltpu.make_async_copy(buf.at[i], dst.at[sample], rsem.at[sample]).start()

        @pl.when(i != j)
        def _():
            remote(
                buf.at[i],
                dst.at[sample],
                ssem.at[i],
                rsem.at[sample],
                (xh, z, y, i // 2, i % 2),
            ).start()

    def done_part(buf, ssem):
        def one(i, carry):
            @pl.when(i != j)
            def _():
                landed(buf.at[i], ssem.at[i])

            return carry

        lax.fori_loop(0, 4, one, 0)

    up = (xh, z, (y + 1) % 4, xl, co)
    down = (xh, z, (y + 3) % 4, xl, co)
    across = (xh, z, 3 - y, xl, co)
    encoder = y < 2

    def give_left():
        def one(i, carry):
            send_part(L, i, LB, lp_s, lp_r)
            return carry

        lax.fori_loop(0, 4, one, 0)

    def stacked(ref, kind):
        return jnp.concatenate([ref[m, kind] for m in range(MB)], axis=0)

    def order_left():
        col = iota((1, 2 * NZ * 24), 1)
        block, off = col // 24, col % 24
        first = (block % 2) * (C // 2) + (block // 2) * 20
        row = iota((C, 1), 0)
        low = jnp.where(off < 20, first + off, -1)
        high = jnp.where(off >= 4, first + off - 4, -1)
        s_low[...] = jnp.where(row == low, 1.0, 0.0).astype(BF16)
        s_high[...] = jnp.where(row == high, 1.0, 0.0).astype(BF16)
        for m in range(MB):
            landed(LB.at[m], lp_r.at[m])
        LP[0] = dot(stacked(LB, 0), s_low[...]).astype(BF16)
        LP[1] = dot(stacked(LB, 1), s_high[...]).astype(BF16)
        LP[2] = dot(stacked(LB, 2), s_low[...]).astype(BF16)

    @pl.when(encoder)
    def _():
        @pl.when(worker)
        def _():
            cond = condition()
            wait_weights(0)
            wait_weights(1)

            @pl.when(y == 0)
            def _():
                cur[...] = xbuf[...].astype(F32)

            @pl.when(y == 1)
            def _():
                landed(xin, hop_r.at[0])
                cur[...] = xin[...].astype(F32)

            def step(i, carry):
                result = activate(i, cur[...], cond)
                L[i, 2] = result
                cur[...] = result.astype(F32)
                return carry

            lax.fori_loop(0, 4, step, 0)
            remote(L.at[3, 2], xin, hop_s.at[0], hop_r.at[0], up).start()

        @pl.when(jnp.logical_not(worker))
        def _():
            wait_weights(0)
            wait_weights(1)

        @pl.when(y == 0)
        def _():
            relay_weights(2)

        wait_weights(2)

        @pl.when(worker)
        def _():
            def give_skip(n, carry):
                i = 3 - n
                skout[i] = dot(L[i, 2], W[2, i]).astype(BF16)
                remote(
                    skout.at[i], L.at[3 - i, 2], sk_s.at[i], sk_r.at[3 - i], across
                ).start()
                return carry

            lax.fori_loop(0, 4, give_skip, 0)
            give_left()

        order_left()

        @pl.when(worker)
        def _():
            def skip_back(i):
                landed(R.at[i, 2], q_r.at[i])
                pre[i] = dot_rhs_t(R[i, 2], W[2, i])

            @pl.when(y == 0)
            def _():
                def one(i, carry):
                    skip_back(i)
                    return carry

                lax.fori_loop(0, 4, one, 0)

            landed(din, hop_r.at[1])
            cur[...] = din[...].astype(F32)

            def step_back(n, carry):
                i = 3 - n

                @pl.when(y == 1)
                def _():
                    skip_back(i)

                d_full = cur[...] + pre[i]
                d_low = back(i, d_full.astype(BF16), d_full)
                send_part(R, i, RB, rp_s, rp_r)
                cur[...] = d_low.astype(F32)
                return carry

            lax.fori_loop(0, 4, step_back, 0)

            @pl.when(y == 1)
            def _():
                xout[...] = cur[...].astype(BF16)
                remote(xout, din, hop_s.at[1], hop_r.at[1], down).start()

    @pl.when(jnp.logical_not(encoder))
    def _():
        wait_weights(0)
        wait_weights(1)
        wait_weights(2)

        @pl.when(worker)
        def _():
            cond = condition()

            def skip_in(i):
                landed(L.at[i, 2], sk_r.at[i])
                pre[i] = dot(L[i, 2], W[2, i])

            @pl.when(y == 3)
            def _():
                def one(i, carry):
                    skip_in(i)
                    return carry

                lax.fori_loop(0, 4, one, 0)

            landed(xin, hop_r.at[0])
            cur[...] = xin[...].astype(F32)

            def step(i, carry):
                @pl.when(y == 2)
                def _():
                    skip_in(i)

                cur[...] = activate(i, cur[...] + pre[i], cond).astype(F32)
                return carry

            lax.fori_loop(0, 4, step, 0)

            @pl.when(y == 2)
            def _():
                xout[...] = cur[...].astype(BF16)
                remote(xout, xin, hop_s.at[0], hop_r.at[0], up).start()

            give_left()

        @pl.when(y == 2)
        def _():
            order_left()

        @pl.when(worker)
        def _():
            @pl.when(y == 3)
            def _():
                cur[...] = dbuf[...].astype(F32)

            @pl.when(y == 2)
            def _():
                landed(din, hop_r.at[1])
                cur[...] = din[...].astype(F32)

            def step_back(n, carry):
                i = 3 - n
                d_full = cur[...]
                g = back(i, d_full.astype(BF16), d_full)
                R[i, 2] = g
                cur[...] = g.astype(F32)
                send_part(R, i, RB, rp_s, rp_r)
                return carry

            lax.fori_loop(0, 4, step_back, 0)
            remote(R.at[0, 2], din, hop_s.at[1], hop_r.at[1], down).start()

            def give_q(i, carry):
                skout[i] = dot_rhs_t(R[i, 2], W[2, i]).astype(BF16)
                remote(
                    skout.at[i], R.at[3 - i, 2], q_s.at[i], q_r.at[3 - i], across
                ).start()
                return carry

            lax.fori_loop(0, 4, give_q, 0)

        @pl.when(y == 3)
        def _():
            order_left()

    for m in range(MB):
        landed(RB.at[m], rp_r.at[m])
    grads = [dot_lhs_t(LP[kind], stacked(RB, kind)) for kind in range(3)]
    for c in range(NZ):
        for h in range(2):
            g_in, g_out, g_skip = (g[48 * c + 24 * h : 48 * c + 24 * h + 24] for g in grads)
            pm[c, 64 * h : 64 * h + 16] = g_in[:16]
            pm[c, 64 * h + 16 : 64 * h + 24] = g_in[16:] + g_out[:8]
            pm[c, 64 * h + 24 : 64 * h + 40] = g_out[8:]
            pm[c, 64 * h + 40 : 64 * h + 64] = g_skip

    half = NZ // 2
    other = 1 - xh

    def at(side, step):
        return (side, (z + step + NZ) % NZ, y, xl, co)

    def rows_of(h):
        return pl.ds(pl.multiple_of(64 * h, 64), 64)

    cross[...] = pm[z, rows_of(other)].astype(BF16)
    remote(cross, fin.at[4], fin_s.at[4], fin_r.at[4], at(other, 0)).start()

    def hop(way, t, first):
        sbuf, rbuf, ssem, rsem = ((sbp, rbp, sps, rps), (sbm, rbm, sms, rms))[way]
        chunk = ((z + half - t) if way == 0 else (z - half + 1 + t + NZ)) % NZ
        for k in range(4):
            rows = pl.ds(32 * k, 32)
            total = pm[chunk, 32 * k : 32 * k + 32]
            if not first:
                landed(rbuf.at[t - 1, rows], rsem.at[t - 1, k])
                total = total + rbuf[t - 1, 32 * k : 32 * k + 32].astype(F32)
            sbuf[t, 32 * k : 32 * k + 32] = total.astype(BF16)
            remote(
                sbuf.at[t, rows],
                rbuf.at[t, rows],
                ssem.at[t, k],
                rsem.at[t, k],
                at(xh, 1 - 2 * way),
            ).start()

    def last_hop(way, t):
        rbuf, rsem, buf = ((rbp, rps, lastp), (rbm, rms, lastm))[way]
        for k in range(4):
            landed(rbuf.at[t - 1, pl.ds(32 * k, 32)], rsem.at[t - 1, k])
        chunk = (z + 1 - 2 * way + NZ) % NZ
        buf[...] = (pm[chunk] + rbuf[t - 1].astype(F32)).astype(BF16)
        for n, side in enumerate((other, xh)):
            slot = 2 * way + n
            remote(
                buf.at[rows_of(side)],
                fin.at[slot],
                fin_s.at[slot],
                fin_r.at[slot],
                at(side, 1 - 2 * way),
            ).start()

    hop(0, 0, True)
    hop(1, 0, True)

    def ring_step(t, carry):
        hop(0, t, False)
        hop(1, t, False)
        return carry

    lax.fori_loop(1, half - 2, ring_step, 0)
    hop(0, half - 2, False)
    last_hop(1, half - 2)
    last_hop(0, half - 1)
    own = pm[z, rows_of(xh)]
    for slot in (4, 3, 2):
        landed(fin.at[slot], fin_r.at[slot])
        own = own + fin[slot].astype(F32)
    out_a[...] = own[:60].reshape(60, 1, C)
    for slot in (1, 0):
        landed(fin.at[slot], fin_r.at[slot])
    rest = fin[0].astype(F32) + fin[1].astype(F32)
    out_b[...] = rest[:60].reshape(60, 1, C)

    chain_sent()
    landed(cross, fin_s.at[4])
    for slot in range(4):
        landed(cross, fin_s.at[slot])

    def left_ring(t, carry):
        for k in range(4):
            landed(sbp.at[0, pl.ds(0, 32)], sps.at[t, k])
        return carry

    lax.fori_loop(0, half - 1, left_ring, 0)

    def left_ring_back(t, carry):
        for k in range(4):
            landed(sbm.at[0, pl.ds(0, 32)], sms.at[t, k])
        return carry

    lax.fori_loop(0, half - 2, left_ring_back, 0)


def on_device(features, timesteps, text_ids, text_table, w_in, w_out, w_skip, cotangent):
    dma = pltpu.SemaphoreType.DMA
    half = NZ // 2

    def bf(*shape):
        return pltpu.VMEM(shape, BF16)

    def f32(*shape):
        return pltpu.VMEM(shape, F32)

    block = (ROWS, C)
    scratch = [
        pltpu.VMEM(text_ids.shape[::-1], jnp.int32),
        bf(*text_table.shape),
        bf(3, 4, C, C),
        f32(*block),
        bf(*block),
        bf(*block),
        bf(*block),
        bf(*block),
        bf(*block),
        bf(4, *block),
        f32(4, *block),
        bf(4, 3, *block),
        bf(4, 3, *block),
        f32(4, *block),
        f32(4, 8, C),
        bf(MB, 3, *block),
        bf(MB, 3, *block),
        bf(3, MB * ROWS, 2 * NZ * 24),
        bf(C, C),
        bf(C, 2 * NZ * 24),
        bf(C, 2 * NZ * 24),
        f32(2 * MB, 16, C),
        bf(2 * MB, 16, C),
        bf(8, 16, C),
        bf(16, C),
        bf(4, 16, C),
        f32(NZ, 1, C),
        f32(NZ, 1, C),
        f32(NZ, 128, C),
        bf(half - 1, 128, C),
        bf(half - 1, 128, C),
        bf(half - 2, 128, C),
        bf(half - 2, 128, C),
        bf(128, C),
        bf(128, C),
        bf(64, C),
        bf(5, 64, C),
        dma((4,)),
        dma((3,)),
        dma((3,)),
        dma((3,)),
        dma((3, 2)),
        dma((3, 2)),
        dma((3, 2)),
        dma((3, 2)),
        dma((2 * MB,)),
        dma((8,)),
        dma((4,)),
        dma((4,)),
        dma((NZ,)),
        dma((NZ,)),
        dma((2,)),
        dma((2,)),
        dma((4,)),
        dma((4,)),
        dma((4,)),
        dma((4,)),
        dma((4,)),
        dma((MB,)),
        dma((4,)),
        dma((MB,)),
        dma((half - 1, 4)),
        dma((half - 1, 4)),
        dma((half - 2, 4)),
        dma((half - 2, 4)),
        dma((5,)),
        dma((5,)),
    ]
    vmem = pl.BlockSpec(memory_space=pltpu.VMEM)
    hbm = pl.BlockSpec(memory_space=pl.ANY)
    sums = jax.ShapeDtypeStruct((60, 1, C), F32)
    first, second = pl.pallas_call(
        kernel,
        out_shape=(sums, sums),
        in_specs=[pl.BlockSpec(memory_space=pltpu.SMEM)] + [hbm] * 7,
        out_specs=(vmem, vmem),
        scratch_shapes=scratch,
        compiler_params=pltpu.CompilerParams(
            collective_id=0, has_side_effects=True, vmem_limit_bytes=56 * 2**20
        ),
        name="unet_step",
    )(timesteps, features, text_ids.T, text_table, w_in, w_out, w_skip, cotangent)
    return tuple(
        jnp.transpose(first[20 * k : 20 * k + 20] + second[20 * k : 20 * k + 20], (1, 0, 2))
        for k in range(3)
    )


def solution(mesh):
    split_mesh = Mesh(mesh.devices.reshape(2, NZ, 4, 2, 2), AXES)
    weight = P(SEG, None, None)
    return jax.shard_map(
        on_device,
        mesh=split_mesh,
        in_specs=(
            P(DP, None),
            P(DP),
            P(),
            P(DP + SEG, None),
            weight,
            weight,
            weight,
            P(DP, None),
        ),
        out_specs=(P(SEG, DP, None),) * 3,
        check_vma=False,
    )
```

time: 160 us -> 143 us (0.89)
  Pallas kernels: 153 us -> 140 us
  local copies, waits for them, and re-layouts: 3.66 us -> 0 us
    pallas_call x1, Pallas kernels: 153 us -> 140 us  [on_device(): pl.pallas_call(kernel, out_shape=(sums, sums), in_specs=[pl.BlockSpec(mem...]
    unnamed x6 -> x0, local copies, waits for them, and re-layouts: 2.74 us -> none
    transpose x0 -> x1, other arithmetic: none -> 1.73 us  [on_device(): jnp.transpose(first[20 * k:20 * k + 20] + second[20 * k:20 * k + 20], (1,...]
where the time goes in v2:
time: 143 us; the launch traced here: 142 us
  Pallas kernels  140 us (98%)
  other arithmetic  1.73 us (1%)
    pallas_call x1, Pallas kernels, on_device(): pl.pallas_call(kernel, out_shape=(sums, sums), in_specs=[pl.BlockSpec(mem...  140 us

profile of v2, /device:TPU:6, one launch (start us, length us, event | category | flops | bytes accessed | tf_op | source)
XLA Modules:
  0.0 142.4 jit_solution(15110989843890979915)
XLA Ops:
  0.6 140.0 %unet_step.1 = (f32[60,1,640]{2,1,0:T(1,128)}, f32[60,1,640]{2,1,0:T(1,128)}) custom-call(s32[3]{0:T(128)} %steps.1, bf16[192,640]{1,0:T(8,128)(2,1)} %feat.1, s32[64,96]{1,0:T(8,128)} %bitcast.7, bf16[32,640]{1,0:T(8,128)(2,1)} %table_in.1, bf16[1,640,640]{2,1,0:T(8,128)(2,1)} %w_in.1, bf16[1,640,640]{2,1,0:T(8,128)(2,1)} %w_out.1, ...), custom_call_target="tpu_custom_call" | custom-call | tf_op jit(solution)/shard_map/unet_step/pallas_call | solution.py:819
  140.7 1.7 %add_bitcast_fusion = (f32[1,20,640]{2,0,1:T(1,128)}, f32[1,20,640]{2,0,1:T(1,128)}, f32[1,20,640]{2,0,1:T(1,128)}) fusion(f32[60,1,640]{2,1,0:T(1,128)} %get-tuple-element.6, f32[60,1,640]{2,1,0:T(1,128)} %get-tuple-element.5), kind=kLoop, calls=%fused_computation | loop fusion | flops 38400 | bytes 460800 | tf_op jit(solution)/shard_map/transpose | solution.py:831

commit v3 on v2

--- a/solution.py
+++ b/solution.py
@@ -26,10 +26,6 @@
     return jnp.dot(a, b, preferred_element_type=F32)
 
 
-def dot_rhs_t(a, b):
-    return lax.dot_general(a, b, (((1,), (1,)), ((), ())), preferred_element_type=F32)
-
-
 def dot_lhs_t(a, b):
     return lax.dot_general(a, b, (((0,), (0,)), ((), ())), preferred_element_type=F32)
 
@@ -60,12 +56,15 @@
     return out
 
 
-def normalize(v, group_matrix):
-    (mean,) = group_means([jnp.sum(v, axis=0, keepdims=True)], 3, group_matrix)
-    shifted = v - mean
-    (var,) = group_means([jnp.sum(shifted * shifted, axis=0, keepdims=True)], 2, group_matrix)
-    inv = lax.rsqrt(var + EPSILON)
-    return shifted * inv, inv
+def normalize(v, about, group_matrix):
+    v = v - about
+    mean, square = group_means(
+        [jnp.sum(v, axis=0, keepdims=True), jnp.sum(v * v, axis=0, keepdims=True)],
+        3,
+        group_matrix,
+    )
+    inv = lax.rsqrt(jnp.maximum(square - mean * mean, 0.0) + EPSILON)
+    return (v - mean) * inv, inv, about + mean
 
 
 def normalize_back(v, normed, inv, group_matrix):
@@ -95,6 +94,8 @@
     ids,
     table,
     W,
+    WT,
+    shift,
     cur,
     xbuf,
     dbuf,
@@ -159,6 +160,7 @@
     rms,
     fin_s,
     fin_r,
+    reach,
 ):
     xh, z, y = lax.axis_index("xh"), lax.axis_index("z"), lax.axis_index("y")
     xl, co = lax.axis_index("xl"), lax.axis_index("co")
@@ -198,11 +200,9 @@
     for side in (1, NZ - 1):
         greet((1 - xh, (z + side) % NZ, y, xl, co))
 
-    def greet_z(d, carry):
+    for d in (1, 2, 3, 4):
         greet((xh, (z + d) % NZ, y, xl, co))
-        return carry
-
-    lax.fori_loop(1, NZ, greet_z, 0)
+        greet((xh, (z + NZ - d) % NZ, y, xl, co))
 
     landed(ids, in_sem.at[2])
     landed(table, in_sem.at[3])
@@ -227,37 +227,90 @@
     p0f[...] = part.reshape(2 * MB, 16, C)
     p0b[...] = p0f[...].astype(BF16)
 
-    pl.semaphore_wait(barrier, 7 + 3 + 2 + NZ - 1)
+    pl.semaphore_wait(barrier, 7 + 3 + 2 + 8)
+    for d in (4, NZ - 4):
+        pl.semaphore_signal(
+            reach, inc=1, device_id=(xh, (z + d) % NZ, y, xl, co), device_id_type=MESH
+        )
 
     core_dev = (xh, z, y, xl, 1 - co)
     x_devs = ((xh, z, y, 1 - xl, co), (1 - xh, z, y, 1 - xl, co))
-    halves = (pl.ds(0, C // 2), pl.ds(C // 2, C // 2))
+    quarter = C // 4
+    quarters = [[pl.ds((2 * h + n) * quarter, quarter) for n in range(2)] for h in range(2)]
     far = 2 * (1 - xl) + co
 
-    def start_weights(kind):
+    def start_weights(kind, n):
         for h in range(2):
+            rows = quarters[h][n]
             remote(
-                weights[kind].at[0, halves[h]],
-                W.at[kind, j, halves[h]],
-                wxs.at[kind, h],
-                wxr.at[kind, h],
+                weights[kind].at[0, rows],
+                W.at[kind, j, rows],
+                wxs.at[kind, h, n],
+                wxr.at[kind, h, n],
                 x_devs[h],
             ).start()
-        remote(
-            weights[kind].at[0], W.at[kind, j], wcs.at[kind], wcr.at[kind], core_dev
-        ).start()
+        if n == 1:
+            remote(
+                weights[kind].at[0], W.at[kind, j], wcs.at[kind], wcr.at[kind], core_dev
+            ).start()
 
     def relay_weights(kind):
-        for h in range(2):
-            block = W.at[kind, far, halves[h]]
-            landed(block, wxr.at[kind, h])
-            remote(block, block, wfs.at[kind, h], wfr.at[kind, h], core_dev).start()
+        for n in range(2):
+            for h in range(2):
+                block = W.at[kind, far, quarters[h][n]]
+                landed(block, wxr.at[kind, h, n])
+                remote(
+                    block, block, wfs.at[kind, h, n], wfr.at[kind, h, n], core_dev
+                ).start()
 
     def wait_weights(kind):
         landed(W.at[kind, 0], wl.at[kind])
         landed(W.at[kind, 0], wcr.at[kind])
         for h in range(2):
-            landed(W.at[kind, 0, halves[h]], wfr.at[kind, h])
+            for n in range(2):
+                landed(W.at[kind, 0, quarters[h][n]], wfr.at[kind, h, n])
+
+    def startup_sent():
+        for b in range(2 * MB):
+            bx, bj = b // MB, b % MB
+
+            @pl.when(p != 4 * bx + bj)
+            def _():
+                landed(p0b.at[0], c1s_sem.at[b])
+
+        @pl.when(worker)
+        def _():
+            for d in range(1, 4):
+                landed(c2s, c2s_sem.at[d])
+
+            def given(d, carry):
+                q = (z + d) % NZ
+                landed(c3s.at[q], c3s_sem.at[q])
+                return carry
+
+            lax.fori_loop(1, NZ, given, 0)
+
+        for kind in range(3):
+            landed(W.at[kind, 0], wcs.at[kind])
+            for h in range(2):
+                for n in range(2):
+                    landed(W.at[kind, 0, quarters[h][n]], wxs.at[kind, h, n])
+                    landed(W.at[kind, 0, quarters[h][n]], wfs.at[kind, h, n])
+
+    def condition():
+        lane = iota((1, C), 1)
+        half_width = C // 2
+        k = jnp.where(lane < half_width, lane, lane - half_width).astype(F32)
+        freqs = jnp.exp(-math.log(10000.0) * k / half_width)
+        angles = steps[sample].astype(F32) * freqs
+        total = jnp.where(lane < half_width, jnp.cos(angles), jnp.sin(angles)) + c3s[z]
+
+        def add(d, acc):
+            q = (z + d) % NZ
+            landed(c3.at[q], c3r_sem.at[q])
+            return acc + c3[q]
+
+        return lax.fori_loop(1, NZ, add, total)
 
     for b in range(2 * MB):
         bx, bj = b // MB, b % MB
@@ -272,8 +325,7 @@
                 (bx, z, y, bj // 2, bj % 2),
             ).start()
 
-    start_weights(0)
-    start_weights(1)
+    start_weights(0, 0)
     gmat[...] = jnp.where(
         iota((C, 1), 0) // (C // GROUPS) == iota((1, C), 1) // (C // GROUPS), 1.0, 0.0
     ).astype(BF16)
@@ -290,10 +342,12 @@
             remote(
                 c2s, c2.at[y], c2s_sem.at[d], c2r_sem.at[y], (xh, z, (y + d) % 4, xl, co)
             ).start()
+        start_weights(0, 1)
         for d in range(1, 4):
             q = (y + d) % 4
             landed(c2.at[q], c2r_sem.at[q])
             acc = acc + c2[q].astype(F32)
+        pl.semaphore_wait(reach, 2)
         for r in range(NZ):
             c3s[r] = acc[r : r + 1]
 
@@ -306,58 +360,25 @@
 
         lax.fori_loop(1, NZ, give, 0)
 
-    start_weights(2)
+    @pl.when(jnp.logical_not(worker))
+    def _():
+        start_weights(0, 1)
+        pl.semaphore_wait(reach, 2)
+
+    start_weights(1, 0)
+    start_weights(1, 1)
     relay_weights(0)
     relay_weights(1)
-
-    @pl.when(y > 0)
+    start_weights(2, 0)
+    start_weights(2, 1)
+
+    @pl.when(y >= 2)
     def _():
         relay_weights(2)
 
     landed(xbuf, in_sem.at[0])
     landed(dbuf, in_sem.at[1])
 
-    def condition():
-        lane = iota((1, C), 1)
-        half_width = C // 2
-        k = jnp.where(lane < half_width, lane, lane - half_width).astype(F32)
-        freqs = jnp.exp(-math.log(10000.0) * k / half_width)
-        angles = steps[sample].astype(F32) * freqs
-        total = jnp.where(lane < half_width, jnp.cos(angles), jnp.sin(angles)) + c3s[z]
-
-        def add(d, acc):
-            q = (z + d) % NZ
-            landed(c3.at[q], c3r_sem.at[q])
-            return acc + c3[q]
-
-        return lax.fori_loop(1, NZ, add, total)
-
-
-    def startup_sent():
-        for b in range(2 * MB):
-            bx, bj = b // MB, b % MB
-
-            @pl.when(p != 4 * bx + bj)
-            def _():
-                landed(p0b.at[0], c1s_sem.at[b])
-
-        @pl.when(worker)
-        def _():
-            for d in range(1, 4):
-                landed(c2s, c2s_sem.at[d])
-
-            def given(d, carry):
-                q = (z + d) % NZ
-                landed(c3s.at[q], c3s_sem.at[q])
-                return carry
-
-            lax.fori_loop(1, NZ, given, 0)
-
-        for kind in range(3):
-            landed(W.at[kind, 0], wcs.at[kind])
-            for h in range(2):
-                landed(W.at[kind, 0, halves[h]], wxs.at[kind, h])
-                landed(W.at[kind, 0, halves[h]], wfs.at[kind, h])
 
     def chain_sent():
         startup_sent()
@@ -389,7 +410,7 @@
                 landed(xout, hop_s.at[1])
 
     def activate(i, v, cond):
-        normed, inv = normalize(v, gmat[...])
+        normed, inv, shift[...] = normalize(v, shift[...], gmat[...])
         low = normed.astype(BF16)
         L[i, 0] = low
         inv_std[i] = jnp.broadcast_to(inv, (8, C))
@@ -400,11 +421,14 @@
         sp[i] = sig * (1.0 + act * (1.0 - sig))
         return (v + dot(hidden, W[1, i])).astype(BF16)
 
+    def start_shift(v):
+        (shift[...],) = group_means([jnp.sum(v, axis=0, keepdims=True)], 3, gmat[...])
+
     def back(i, d_low, d_full):
         R[i, 1] = d_low
-        e = (dot_rhs_t(d_low, W[1, i]) * sp[i]).astype(BF16)
+        e = (dot(d_low, WT[1, i]) * sp[i]).astype(BF16)
         R[i, 0] = e
-        v = dot_rhs_t(e, W[0, i])
+        v = dot(e, WT[0, i])
         g = normalize_back(v, L[i, 0].astype(F32), inv_std[i, 0:1], gmat[...])
         return (d_full + g).astype(BF16)
 
@@ -437,6 +461,14 @@
     down = (xh, z, (y + 3) % 4, xl, co)
     across = (xh, z, 3 - y, xl, co)
     encoder = y < 2
+
+    def transpose_weights():
+        def one(i, carry):
+            for kind in range(3):
+                WT[kind, i] = W[kind, i].T
+            return carry
+
+        lax.fori_loop(0, 4, one, 0)
 
     def give_left():
         def one(i, carry):
@@ -459,9 +491,8 @@
         s_high[...] = jnp.where(row == high, 1.0, 0.0).astype(BF16)
         for m in range(MB):
             landed(LB.at[m], lp_r.at[m])
-        LP[0] = dot(stacked(LB, 0), s_low[...]).astype(BF16)
-        LP[1] = dot(stacked(LB, 1), s_high[...]).astype(BF16)
-        LP[2] = dot(stacked(LB, 2), s_low[...]).astype(BF16)
+        for kind, order in enumerate((s_low, s_high, s_low)):
+            LP[kind] = dot(stacked(LB, kind), order[...]).astype(BF16).T
 
     @pl.when(encoder)
     def _():
@@ -479,6 +510,8 @@
             def _():
                 landed(xin, hop_r.at[0])
                 cur[...] = xin[...].astype(F32)
+
+            start_shift(cur[...])
 
             def step(i, carry):
                 result = activate(i, cur[...], cond)
@@ -494,10 +527,7 @@
             wait_weights(0)
             wait_weights(1)
 
-        @pl.when(y == 0)
-        def _():
-            relay_weights(2)
-
+        relay_weights(2)
         wait_weights(2)
 
         @pl.when(worker)
@@ -517,9 +547,11 @@
 
         @pl.when(worker)
         def _():
+            transpose_weights()
+
             def skip_back(i):
                 landed(R.at[i, 2], q_r.at[i])
-                pre[i] = dot_rhs_t(R[i, 2], W[2, i])
+                pre[i] = dot(R[i, 2], WT[2, i])
 
             @pl.when(y == 0)
             def _():
@@ -561,6 +593,7 @@
         @pl.when(worker)
         def _():
             cond = condition()
+            transpose_weights()
 
             def skip_in(i):
                 landed(L.at[i, 2], sk_r.at[i])
@@ -577,8 +610,14 @@
             landed(xin, hop_r.at[0])
             cur[...] = xin[...].astype(F32)
 
+            @pl.when(y == 2)
+            def _():
+                skip_in(0)
+
+            start_shift(cur[...] + pre[0])
+
             def step(i, carry):
-                @pl.when(y == 2)
+                @pl.when(jnp.logical_and(y == 2, i > 0))
                 def _():
                     skip_in(i)
 
@@ -622,7 +661,7 @@
             remote(R.at[0, 2], din, hop_s.at[1], hop_r.at[1], down).start()
 
             def give_q(i, carry):
-                skout[i] = dot_rhs_t(R[i, 2], W[2, i]).astype(BF16)
+                skout[i] = dot(R[i, 2], WT[2, i]).astype(BF16)
                 remote(
                     skout.at[i], R.at[3 - i, 2], q_s.at[i], q_r.at[3 - i], across
                 ).start()
@@ -636,7 +675,7 @@
 
     for m in range(MB):
         landed(RB.at[m], rp_r.at[m])
-    grads = [dot_lhs_t(LP[kind], stacked(RB, kind)) for kind in range(3)]
+    grads = [dot(LP[kind], stacked(RB, kind)) for kind in range(3)]
     for c in range(NZ):
         for h in range(2):
             g_in, g_out, g_skip = (g[48 * c + 24 * h : 48 * c + 24 * h + 24] for g in grads)
@@ -657,23 +696,24 @@
     cross[...] = pm[z, rows_of(other)].astype(BF16)
     remote(cross, fin.at[4], fin_s.at[4], fin_r.at[4], at(other, 0)).start()
 
-    def hop(way, t, first):
-        sbuf, rbuf, ssem, rsem = ((sbp, rbp, sps, rps), (sbm, rbm, sms, rms))[way]
-        chunk = ((z + half - t) if way == 0 else (z - half + 1 + t + NZ)) % NZ
+    def hop(ways, t, first):
         for k in range(4):
             rows = pl.ds(32 * k, 32)
-            total = pm[chunk, 32 * k : 32 * k + 32]
-            if not first:
-                landed(rbuf.at[t - 1, rows], rsem.at[t - 1, k])
-                total = total + rbuf[t - 1, 32 * k : 32 * k + 32].astype(F32)
-            sbuf[t, 32 * k : 32 * k + 32] = total.astype(BF16)
-            remote(
-                sbuf.at[t, rows],
-                rbuf.at[t, rows],
-                ssem.at[t, k],
-                rsem.at[t, k],
-                at(xh, 1 - 2 * way),
-            ).start()
+            for way in ways:
+                sbuf, rbuf, ssem, rsem = ((sbp, rbp, sps, rps), (sbm, rbm, sms, rms))[way]
+                chunk = ((z + half - t) if way == 0 else (z - half + 1 + t + NZ)) % NZ
+                total = pm[chunk, 32 * k : 32 * k + 32]
+                if not first:
+                    landed(rbuf.at[t - 1, rows], rsem.at[t - 1, k])
+                    total = total + rbuf[t - 1, 32 * k : 32 * k + 32].astype(F32)
+                sbuf[t, 32 * k : 32 * k + 32] = total.astype(BF16)
+                remote(
+                    sbuf.at[t, rows],
+                    rbuf.at[t, rows],
+                    ssem.at[t, k],
+                    rsem.at[t, k],
+                    at(xh, 1 - 2 * way),
+                ).start()
 
     def last_hop(way, t):
         rbuf, rsem, buf = ((rbp, rps, lastp), (rbm, rms, lastm))[way]
@@ -691,16 +731,14 @@
                 at(side, 1 - 2 * way),
             ).start()
 
-    hop(0, 0, True)
-    hop(1, 0, True)
+    hop((0, 1), 0, True)
 
     def ring_step(t, carry):
-        hop(0, t, False)
-        hop(1, t, False)
+        hop((0, 1), t, False)
         return carry
 
     lax.fori_loop(1, half - 2, ring_step, 0)
-    hop(0, half - 2, False)
+    hop((0,), half - 2, False)
     last_hop(1, half - 2)
     last_hop(0, half - 1)
     own = pm[z, rows_of(xh)]
@@ -748,6 +786,8 @@
         pltpu.VMEM(text_ids.shape[::-1], jnp.int32),
         bf(*text_table.shape),
         bf(3, 4, C, C),
+        bf(3, 4, C, C),
+        f32(1, C),
         f32(*block),
         bf(*block),
         bf(*block),
@@ -762,7 +802,7 @@
         f32(4, 8, C),
         bf(MB, 3, *block),
         bf(MB, 3, *block),
-        bf(3, MB * ROWS, 2 * NZ * 24),
+        bf(3, 2 * NZ * 24, MB * ROWS),
         bf(C, C),
         bf(C, 2 * NZ * 24),
         bf(C, 2 * NZ * 24),
@@ -786,10 +826,10 @@
         dma((3,)),
         dma((3,)),
         dma((3,)),
-        dma((3, 2)),
-        dma((3, 2)),
-        dma((3, 2)),
-        dma((3, 2)),
+        dma((3, 2, 2)),
+        dma((3, 2, 2)),
+        dma((3, 2, 2)),
+        dma((3, 2, 2)),
         dma((2 * MB,)),
         dma((8,)),
         dma((4,)),
@@ -812,6 +852,7 @@
         dma((half - 2, 4)),
         dma((5,)),
         dma((5,)),
+        pltpu.SemaphoreType.REGULAR,
     ]
     vmem = pl.BlockSpec(memory_space=pltpu.VMEM)
     hbm = pl.BlockSpec(memory_space=pl.ANY)

time: 143 us -> 137 us (0.958)
  Pallas kernels: 140 us -> 135 us
    pallas_call x1, Pallas kernels: 140 us -> 135 us  [on_device(): pl.pallas_call(kernel, out_shape=(sums, sums), in_specs=[pl.BlockSpec(mem...]
where the time goes in v3:
time: 137 us
  Pallas kernels  135 us (99%)
  other arithmetic  1.73 us (1%)
    pallas_call x1, Pallas kernels, on_device(): pl.pallas_call(kernel, out_shape=(sums, sums), in_specs=[pl.BlockSpec(mem...  135 us

profile of v3, /device:TPU:6, one launch (start us, length us, event | category | flops | bytes accessed | tf_op | source)
XLA Modules:
  0.0 136.9 jit_solution(14596138188138502100)
XLA Ops:
  0.6 134.5 %unet_step.1 = (f32[60,1,640]{2,1,0:T(1,128)}, f32[60,1,640]{2,1,0:T(1,128)}) custom-call(s32[3]{0:T(128)} %steps.1, bf16[192,640]{1,0:T(8,128)(2,1)} %feat.1, s32[64,96]{1,0:T(8,128)} %bitcast.7, bf16[32,640]{1,0:T(8,128)(2,1)} %table_in.1, bf16[1,640,640]{2,1,0:T(8,128)(2,1)} %w_in.1, bf16[1,640,640]{2,1,0:T(8,128)(2,1)} %w_out.1, ...), custom_call_target="tpu_custom_call" | custom-call | tf_op jit(solution)/shard_map/unet_step/pallas_call | solution.py:860
  135.2 1.7 %add_bitcast_fusion = (f32[1,20,640]{2,0,1:T(1,128)}, f32[1,20,640]{2,0,1:T(1,128)}, f32[1,20,640]{2,0,1:T(1,128)}) fusion(f32[60,1,640]{2,1,0:T(1,128)} %get-tuple-element.6, f32[60,1,640]{2,1,0:T(1,128)} %get-tuple-element.5), kind=kLoop, calls=%fused_computation | loop fusion | flops 38400 | bytes 460800 | tf_op jit(solution)/shard_map/transpose | solution.py:872

commit v4 on v3

--- a/solution.py
+++ b/solution.py
@@ -106,10 +106,12 @@
     pre,
     L,
     R,
+    R2,
     sp,
     inv_std,
     LB,
     RB,
+    RB2,
     LP,
     gmat,
     s_low,
@@ -154,6 +156,8 @@
     lp_r,
     rp_s,
     rp_r,
+    kp_s,
+    kp_r,
     sps,
     rps,
     sms,
@@ -367,10 +371,14 @@
 
     start_weights(1, 0)
     start_weights(1, 1)
+
+    def start_skip_weights():
+        start_weights(2, 0)
+        start_weights(2, 1)
+
     relay_weights(0)
     relay_weights(1)
-    start_weights(2, 0)
-    start_weights(2, 1)
+    start_skip_weights()
 
     @pl.when(y >= 2)
     def _():
@@ -385,8 +393,9 @@
 
         @pl.when(worker)
         def _():
-            done_part(L, lp_s)
-            done_part(R, rp_s)
+            done_part(L.at[0], lp_s)
+            done_part(R.at[0], rp_s)
+            done_part(R2.at[0], kp_s)
 
             def sent(i, carry):
                 @pl.when(encoder)
@@ -432,26 +441,26 @@
         g = normalize_back(v, L[i, 0].astype(F32), inv_std[i, 0:1], gmat[...])
         return (d_full + g).astype(BF16)
 
-    def send_part(buf, i, dst, ssem, rsem):
+    def send_part(src, dst, i, ssem, rsem):
         @pl.when(i == j)
         def _():
-            pltpu.make_async_copy(buf.at[i], dst.at[sample], rsem.at[sample]).start()
+            pltpu.make_async_copy(src, dst, rsem).start()
 
         @pl.when(i != j)
         def _():
-            remote(
-                buf.at[i],
-                dst.at[sample],
-                ssem.at[i],
-                rsem.at[sample],
-                (xh, z, y, i // 2, i % 2),
-            ).start()
-
-    def done_part(buf, ssem):
+            remote(src, dst, ssem, rsem, (xh, z, y, i // 2, i % 2)).start()
+
+    def send_right(i):
+        send_part(R.at[i], RB.at[sample], i, rp_s.at[i], rp_r.at[sample])
+
+    def send_right_skip(i):
+        send_part(R2.at[i], RB2.at[sample], i, kp_s.at[i], kp_r.at[sample])
+
+    def done_part(like, ssem):
         def one(i, carry):
             @pl.when(i != j)
             def _():
-                landed(buf.at[i], ssem.at[i])
+                landed(like, ssem.at[i])
 
             return carry
 
@@ -472,7 +481,7 @@
 
     def give_left():
         def one(i, carry):
-            send_part(L, i, LB, lp_s, lp_r)
+            send_part(L.at[i], LB.at[sample], i, lp_s.at[i], lp_r.at[sample])
             return carry
 
         lax.fori_loop(0, 4, one, 0)
@@ -494,6 +503,21 @@
         for kind, order in enumerate((s_low, s_high, s_low)):
             LP[kind] = dot(stacked(LB, kind), order[...]).astype(BF16).T
 
+    def each(first, count, fn):
+        def one(i, carry):
+            fn(i)
+            return carry
+
+        lax.fori_loop(first, count, one, 0)
+
+    def give_skip(i):
+        skout[i] = dot(L[i, 2], W[2, i]).astype(BF16)
+        remote(skout.at[i], L.at[3 - i, 2], sk_s.at[i], sk_r.at[3 - i], across).start()
+
+    def give_q(i):
+        skout[i] = dot(R2[i], WT[2, i]).astype(BF16)
+        remote(skout.at[i], R2.at[3 - i], q_s.at[i], q_r.at[3 - i], across).start()
+
     @pl.when(encoder)
     def _():
         @pl.when(worker)
@@ -517,6 +541,7 @@
                 result = activate(i, cur[...], cond)
                 L[i, 2] = result
                 cur[...] = result.astype(F32)
+
                 return carry
 
             lax.fori_loop(0, 4, step, 0)
@@ -532,15 +557,7 @@
 
         @pl.when(worker)
         def _():
-            def give_skip(n, carry):
-                i = 3 - n
-                skout[i] = dot(L[i, 2], W[2, i]).astype(BF16)
-                remote(
-                    skout.at[i], L.at[3 - i, 2], sk_s.at[i], sk_r.at[3 - i], across
-                ).start()
-                return carry
-
-            lax.fori_loop(0, 4, give_skip, 0)
+            each(0, 4, lambda n: give_skip(3 - n))
             give_left()
 
         order_left()
@@ -550,16 +567,16 @@
             transpose_weights()
 
             def skip_back(i):
-                landed(R.at[i, 2], q_r.at[i])
-                pre[i] = dot(R[i, 2], WT[2, i])
+                landed(R2.at[i], q_r.at[i])
+                pre[i] = dot(R2[i], WT[2, i])
 
             @pl.when(y == 0)
             def _():
-                def one(i, carry):
+                def ahead(i):
                     skip_back(i)
-                    return carry
-
-                lax.fori_loop(0, 4, one, 0)
+                    send_right_skip(i)
+
+                each(0, 4, ahead)
 
             landed(din, hop_r.at[1])
             cur[...] = din[...].astype(F32)
@@ -570,10 +587,12 @@
                 @pl.when(y == 1)
                 def _():
                     skip_back(i)
+                    send_right_skip(i)
 
                 d_full = cur[...] + pre[i]
                 d_low = back(i, d_full.astype(BF16), d_full)
-                send_part(R, i, RB, rp_s, rp_r)
+
+                send_right(i)
                 cur[...] = d_low.astype(F32)
                 return carry
 
@@ -601,11 +620,7 @@
 
             @pl.when(y == 3)
             def _():
-                def one(i, carry):
-                    skip_in(i)
-                    return carry
-
-                lax.fori_loop(0, 4, one, 0)
+                each(0, 4, skip_in)
 
             landed(xin, hop_r.at[0])
             cur[...] = xin[...].astype(F32)
@@ -652,30 +667,26 @@
                 i = 3 - n
                 d_full = cur[...]
                 g = back(i, d_full.astype(BF16), d_full)
-                R[i, 2] = g
+                R2[i] = g
                 cur[...] = g.astype(F32)
-                send_part(R, i, RB, rp_s, rp_r)
+                send_right_skip(i)
+                send_right(i)
+
                 return carry
 
             lax.fori_loop(0, 4, step_back, 0)
-            remote(R.at[0, 2], din, hop_s.at[1], hop_r.at[1], down).start()
-
-            def give_q(i, carry):
-                skout[i] = dot(R[i, 2], WT[2, i]).astype(BF16)
-                remote(
-                    skout.at[i], R.at[3 - i, 2], q_s.at[i], q_r.at[3 - i], across
-                ).start()
-                return carry
-
-            lax.fori_loop(0, 4, give_q, 0)
+            remote(R2.at[0], din, hop_s.at[1], hop_r.at[1], down).start()
+            each(0, 4, give_q)
 
         @pl.when(y == 3)
         def _():
             order_left()
 
     for m in range(MB):
+        landed(RB2.at[m], kp_r.at[m])
         landed(RB.at[m], rp_r.at[m])
-    grads = [dot(LP[kind], stacked(RB, kind)) for kind in range(3)]
+    grads = [dot(LP[kind], stacked(RB, kind)) for kind in range(2)]
+    grads.append(dot(LP[2], jnp.concatenate([RB2[m] for m in range(MB)], axis=0)))
     for c in range(NZ):
         for h in range(2):
             g_in, g_out, g_skip = (g[48 * c + 24 * h : 48 * c + 24 * h + 24] for g in grads)
@@ -797,11 +808,13 @@
         bf(4, *block),
         f32(4, *block),
         bf(4, 3, *block),
-        bf(4, 3, *block),
+        bf(4, 2, *block),
+        bf(4, *block),
         f32(4, *block),
         f32(4, 8, C),
         bf(MB, 3, *block),
-        bf(MB, 3, *block),
+        bf(MB, 2, *block),
+        bf(MB, *block),
         bf(3, 2 * NZ * 24, MB * ROWS),
         bf(C, C),
         bf(C, 2 * NZ * 24),
@@ -846,6 +859,8 @@
         dma((MB,)),
         dma((4,)),
         dma((MB,)),
+        dma((4,)),
+        dma((MB,)),
         dma((half - 1, 4)),
         dma((half - 1, 4)),
         dma((half - 2, 4)),

time: 137 us -> 135 us (0.985)
  Pallas kernels: 135 us -> 133 us
    pallas_call x1, Pallas kernels: 135 us -> 133 us  [on_device(): pl.pallas_call(kernel, out_shape=(sums, sums), in_specs=[pl.BlockSpec(mem...]
where the time goes in v4:
time: 135 us
  Pallas kernels  133 us (99%)
  other arithmetic  1.73 us (1%)
    pallas_call x1, Pallas kernels, on_device(): pl.pallas_call(kernel, out_shape=(sums, sums), in_specs=[pl.BlockSpec(mem...  133 us

profile of v4, /device:TPU:6, one launch (start us, length us, event | category | flops | bytes accessed | tf_op | source)
XLA Modules:
  0.0 135.1 jit_solution(1758694375790156743)
XLA Ops:
  0.6 132.7 %unet_step.1 = (f32[60,1,640]{2,1,0:T(1,128)}, f32[60,1,640]{2,1,0:T(1,128)}) custom-call(s32[3]{0:T(128)} %steps.1, bf16[192,640]{1,0:T(8,128)(2,1)} %feat.1, s32[64,96]{1,0:T(8,128)} %bitcast.7, bf16[32,640]{1,0:T(8,128)(2,1)} %table_in.1, bf16[1,640,640]{2,1,0:T(8,128)(2,1)} %w_in.1, bf16[1,640,640]{2,1,0:T(8,128)(2,1)} %w_out.1, ...), custom_call_target="tpu_custom_call" | custom-call | tf_op jit(solution)/shard_map/unet_step/pallas_call | solution.py:875
  133.4 1.7 %add_bitcast_fusion = (f32[1,20,640]{2,0,1:T(1,128)}, f32[1,20,640]{2,0,1:T(1,128)}, f32[1,20,640]{2,0,1:T(1,128)}) fusion(f32[60,1,640]{2,1,0:T(1,128)} %get-tuple-element.6, f32[60,1,640]{2,1,0:T(1,128)} %get-tuple-element.5), kind=kLoop, calls=%fused_computation | loop fusion | flops 38400 | bytes 460800 | tf_op jit(solution)/shard_map/transpose | solution.py:887
